TPU v7x, 512 devices: a whole 4x4x16 slice. The times are simulated.
512 devices in a mesh: rows: 16 (over z), vocab: 32 (over x, y, core).
Axes of the slice: x: 4, y: 4, z: 16, core: 2. Of those that a mesh axis runs over, the one named last changes fastest.
Arguments:
- hidden_held: bfloat16 [32, 1, 128, 8192], P('vocab', None, None, 'rows'), may hold values from -64 to 64, as said below
- head_weight: bfloat16 [8192, 131072], P('rows', 'vocab'), may hold values from -0.44194174 to 0.44194174
- state_table: int32 [24, 4096], P(None, 'vocab'), may hold values from -2147483648 to 2147483646
- row_states: int32 [1, 128], P(None, 'rows'), may hold values from 0 to 23
- owner: int32 [1], replicated, may hold values from 0 to 31
Outputs:
- log_probs: float32 [1, 128, 131072], P(None, 'rows', 'vocab')
- entropy: float32 [1, 128], P(None, 'rows')
Inputs may be any that keep to these rules, and one draw needn't show every extreme that they name: `hidden_held`: rows of a holder that owner does not name are not read.
All inputs are finite; a program needn't handle non-finite values.
Results may differ from a plain program's by a relative error of at most 0.0003.
Values may be sent and summed in bfloat16 or wider, within the bound.
No kernel may reach another device: no remote copies, remote signals or barrier semaphores. Data moves between devices by JAX's collectives and lax.ppermute only.
A program may use at most 64 MiB of HBM per device.

v0:
```python
import jax
import jax.numpy as jnp
from jax import lax
from jax.sharding import PartitionSpec as P


def broadcast(value, axis, source):
    kept = jnp.where(lax.axis_index(axis) == source, value, 0).astype(value.dtype)
    return lax.psum(kept, axis)


def unpack_table(state_table):
    bit_shifts = jnp.arange(32, dtype=jnp.int32)
    flags = jnp.bitwise_and(jnp.right_shift(state_table[:, :, None], bit_shifts), 1)
    return flags.reshape(state_table.shape[0], -1)


def shards(hidden_held, head_weight, state_table, row_states, owner):
    batch_size = hidden_held.shape[2]
    group_count = lax.axis_size("rows")
    share_rows = batch_size // group_count
    mask_bits = unpack_table(state_table).astype(jnp.bfloat16)
    held_rows = broadcast(hidden_held[0, 0], "vocab", owner[0])
    partial_value = jnp.dot(held_rows, head_weight, preferred_element_type=jnp.float32)
    summed_all = lax.psum(partial_value, "rows")
    share_logits = lax.dynamic_slice_in_dim(
        summed_all, lax.axis_index("rows") * share_rows, share_rows, 0
    )
    pieces = [share_logits]
    logits = jnp.stack(pieces)
    onehot = (row_states[:, :, None] == jnp.arange(state_table.shape[0], dtype=jnp.int32)).astype(
        jnp.bfloat16
    )
    allowed = jnp.einsum("mrs,sv->mrv", onehot, mask_bits, preferred_element_type=jnp.float32) > 0.5
    masked = jnp.where(allowed, logits, jnp.float32(-1e30))
    local_max = jnp.max(masked, axis=2)
    row_max = lax.pmax(local_max, "vocab")
    scaled = jnp.where(allowed, jnp.exp(logits - row_max[:, :, None]), jnp.float32(0.0))
    local_total = jnp.sum(scaled, axis=2)
    local_weighted = jnp.sum(jnp.where(allowed, scaled * logits, jnp.float32(0.0)), axis=2)
    total, weighted = lax.psum((local_total, local_weighted), "vocab")
    log_norm = row_max + jnp.log(total)
    log_probs = jnp.where(allowed, logits - log_norm[:, :, None], jnp.float32(0.0))
    entropy = log_norm - weighted / total
    return (log_probs, entropy)


def solution(mesh):
    return jax.shard_map(
        shards,
        mesh=mesh,
        in_specs=(
            P("vocab", None, None, "rows"),
            P("rows", "vocab"),
            P(None, "vocab"),
            P(None, "rows"),
            P(),
        ),
        out_specs=(P(None, "rows", "vocab"), P(None, "rows")),
        check_vma=False,
    )
```

profile of v0, /device:TPU:1, one launch (start us, length us, event | category | flops | bytes accessed | tf_op | source)
XLA Modules:
  0.0 433.0 jit_solution(1058438059669754800)
XLA Ops:
  7.2 0.0 all-reduce.4.cloned.1.call-start
  7.9 0.7 select_bitcast_fusion.1
  8.5 0.0 all-reduce.4.cloned.1.call-update
  8.6 0.0 all-reduce.6.cloned.1.call-start
  8.6 139.0 %all-reduce.4.cloned.1.call-done = bf16[128,512]{1,0:T(8,128)(2,1)} async-done(((bf16[128,512]{1,0:T(8,128)(2,1)}), bf16[128,512]{1,0:T(8,128)(2,1)}) %all-reduce.4.cloned.1.call-update) | async-done | bytes 131088 | tf_op jit(solution)/shard_map/psum | solution.py:9
  147.6 4.3 %fusion.5 = f32[128,4096]{1,0:T(8,128)} fusion(bf16[128,512]{1,0:T(8,128)(2,1)} %all-reduce.4.cloned.1.call-done, bf16[512,4096]{1,0:T(8,128)(2,1)} %param.6), kind=kOutput, calls=%fused_computation.14 | convolution fusion | flops 536870912 | bytes 6422528 | tf_op jit(solution)/shard_map/dot_general | solution.py:24
  152.0 0.0 copy-start
  152.0 0.0 copy-start.1
  152.0 0.0 all-reduce.6.cloned.1.call-update
  152.0 0.7 copy-done
  152.7 0.6 and_convert_fusion
  153.3 0.8 convert_element_type.16
  154.1 133.2 %all-reduce.6.cloned.1.call-done = f32[128,4096]{1,0:T(8,128)} async-done(((f32[128,4096]{1,0:T(8,128)}), f32[128,4096]{1,0:T(8,128)}) %all-reduce.6.cloned.1.call-update) | async-done | bytes 2097168 | tf_op jit(solution)/shard_map/psum | solution.py:25
  287.3 0.0 copy-done.1
  287.3 1.2 select_reduce_fusion.1
  288.6 71.6 %pmax.7 = f32[1,8]{1,0:T(1,128)S(1)} all-reduce(f32[1,8]{1,0:T(1,128)S(1)} %bitcast.25), channel_id=1, replica_groups=mesh['rows'=16,'vocab'=32] {'vocab'}, use_global_device_ids=true, to_apply=%region_3.4 | all-reduce | flops 8 | bytes 64 | tf_op jit(solution)/shard_map/pmax | solution.py:37
  360.1 1.2 select_reduce_fusion
  361.3 62.7 %all-reduce = (f32[1,8]{1,0:T(1,128)S(1)}, f32[1,8]{1,0:T(1,128)S(1)}) all-reduce(f32[1,8]{1,0:T(1,128)S(1)} %bitcast.23, f32[1,8]{1,0:T(1,128)S(1)} %bitcast.22), channel_id=1, replica_groups=mesh['rows'=16,'vocab'=32] {'vocab'}, use_global_device_ids=true, to_apply=%region_5.6 | all-reduce | flops 16 | bytes 128 | tf_op jit(solution)/shard_map/psum | solution.py:41
  424.0 0.5 divide_subtract_fusion
  424.5 1.6 select_bitcast_fusion
Async XLA Ops:
  7.2 140.5 %all-reduce.4.cloned.1.call-start = ((), (), s32[]{:S(2)}) async-start(), calls=%async_computation | async-start | bytes 262144 | tf_op jit(solution)/shard_map/psum | solution.py:9
  8.6 278.8 %all-reduce.6.cloned.1.call-start = ((), (), s32[]{:S(2)}) async-start(), calls=%async_computation.1 | async-start | bytes 4194304 | tf_op jit(solution)/shard_map/psum | solution.py:25
  152.0 0.7 copy-start
  152.0 135.4 %copy-start.1 = (s32[1,8]{1,0:T(1,128)S(1)}, s32[1,8]{1,0:T(1,128)}, u32[]{:S(2)}) copy-start(s32[1,8]{1,0:T(1,128)} %param.8) | copy-start | bytes 100
Sparse Core Ops, SparseCore 0:
  11.8 135.7 all-reduce.3
  152.1 135.1 all-reduce.5
where the time goes:
time: 433 us
  waiting for transfers between devices  272 us (63%)
  blocking collectives  134 us (31%)
  between operations  14.7 us (3%)
  matrix products  5.57 us (1%)
  other arithmetic  4.58 us (1%)
    psum x1, waiting for transfers between devices, broadcast(): return lax.psum(kept, axis)  139 us
    psum x1, waiting for transfers between devices, shards(): summed_all = lax.psum(partial_value, 'rows')  133 us
    pmax x1, blocking collectives, shards(): row_max = lax.pmax(local_max, 'vocab')  71.6 us
    psum x1, blocking collectives, shards(): total, weighted = lax.psum((local_total, local_weighted), 'vocab')  62.7 us
  transfers between devices with their start and end apart: 2, of which 2 were waited for; matrix products, arithmetic and copies ran while one was open for 0% of the time, Pallas kernels for 0%

commit v1 on v0

v1 whole, which is shorter than its diff:
```python
import jax
import jax.numpy as jnp
from jax import lax
from jax.experimental import pallas as pl
from jax.experimental.pallas import tpu as pltpu
from jax.sharding import PartitionSpec as P

N = 4096
HALF = N // 2
TAIL = 128
TILES = 8
WIDE = N // TILES
F32 = jnp.float32
I16 = jnp.int16


def encode(values):
    top = jnp.max(jnp.abs(values), axis=1, keepdims=True)
    k = jnp.ceil(8.0 * jnp.log2(jnp.maximum(top, 1e-30) * (1.0 / 32000.0)))
    return jnp.round(values * jnp.exp2(-0.125 * k)), k


def to_i16(values):
    return values.astype(jnp.int32).astype(I16)


def to_f32(codes):
    return codes.astype(jnp.int32).astype(F32)


def scale_of(codes):
    return jnp.exp2(0.125 * to_f32(codes)[:, :1])


def product_kernel(z_ref, x_ref, w_ref, own_ref, up_ref, down_ref, up2_ref, down2_ref, xp_ref, acc_ref):
    step = pl.program_id(0)

    @pl.when(step == 0)
    def _():
        x = jnp.concatenate([x_ref[8 * c : 8 * c + 8].reshape(128, 128) for c in range(4)], axis=1)
        i = lax.broadcasted_iota(jnp.int32, (128, 128), 0)
        source = lax.broadcasted_iota(jnp.int32, (128, 128), 1)
        b = i >> 5
        piece = (z_ref[0] + jnp.where(b == 3, -1, b) + 4 * ((i >> 3) & 3)) & 15
        chosen = (source == 8 * piece + (i & 7)).astype(F32).astype(jnp.bfloat16)
        xp_ref[...] = jnp.dot(chosen, x, preferred_element_type=F32).astype(jnp.bfloat16)

    acc_ref[step] = jnp.dot(xp_ref[...], w_ref[...], preferred_element_type=F32)

    @pl.when(step == TILES - 1)
    def _():
        def rows(lo, hi):
            return jnp.concatenate([acc_ref[t, lo:hi, :] for t in range(TILES)], axis=1)

        own_ref[...] = rows(0, 32)
        for ref, lo in ((up_ref, 32), (down_ref, 96)):
            q, k = encode(rows(lo, lo + 32))
            ref[:, :N] = to_i16(q)
            ref[:, N:] = to_i16(jnp.broadcast_to(k, (32, TAIL)))
        q, k = encode(rows(64, 96))
        tail = to_i16(jnp.broadcast_to(k, (32, TAIL)))
        up2_ref[:, :HALF] = to_i16(q[:, :HALF])
        up2_ref[:, HALF:] = tail
        down2_ref[:, :HALF] = to_i16(q[:, HALF:])
        down2_ref[:, HALF:] = tail


def product(z, x, w):
    def full(shape):
        return pl.BlockSpec(shape, lambda t: (0,) * len(shape))

    outs = ((32, N), (32, N + TAIL), (32, N + TAIL), (32, HALF + TAIL), (32, HALF + TAIL))
    return pl.pallas_call(
        product_kernel,
        grid=(TILES,),
        in_specs=[
            pl.BlockSpec(memory_space=pltpu.SMEM),
            full(x.shape),
            pl.BlockSpec((w.shape[0], WIDE), lambda t: (0, t)),
        ],
        out_specs=[full(s) for s in outs],
        out_shape=[jax.ShapeDtypeStruct(s, F32 if n == 0 else I16) for n, s in enumerate(outs)],
        scratch_shapes=[
            pltpu.VMEM((128, w.shape[0]), jnp.bfloat16),
            pltpu.VMEM((TILES, 128, WIDE), F32),
        ],
        compiler_params=pltpu.CompilerParams(vmem_limit_bytes=24 * 2**20),
        cost_estimate=pl.CostEstimate(flops=2 * 128 * 512 * N, bytes_accessed=6 * 2**20, transcendentals=0),
    )(z, x, w)


def first_sum_kernel(own_ref, low_ref, high_ref, low2_ref, high2_ref, keep_ref, up_ref, far_ref, down_ref):
    near = (
        own_ref[...]
        + to_f32(low_ref[:, :N]) * scale_of(low_ref[:, N:])
        + to_f32(high_ref[:, :N]) * scale_of(high_ref[:, N:])
    )
    left = to_f32(low2_ref[:, :HALF]) * scale_of(low2_ref[:, HALF:])
    right = to_f32(high2_ref[:, :HALF]) * scale_of(high2_ref[:, HALF:])
    right = jnp.concatenate([right[24:], right[:24]], axis=0)
    total = near + jnp.concatenate([left, right], axis=1)
    keep_ref[...] = total[:8]
    for ref, lo in ((up_ref, 8), (far_ref, 16), (down_ref, 24)):
        q, k = encode(total[lo : lo + 8])
        ref[:, :HALF] = to_i16(jnp.concatenate([q[:, :HALF], q[:, HALF:]], axis=0))
        ref[:, HALF:] = to_i16(jnp.broadcast_to(jnp.concatenate([k, k], axis=0), (16, TAIL)))


def first_sum(*arrays):
    coded = jax.ShapeDtypeStruct((16, HALF + TAIL), I16)
    return pl.pallas_call(
        first_sum_kernel,
        out_shape=[jax.ShapeDtypeStruct((8, N), F32), coded, coded, coded],
        compiler_params=pltpu.CompilerParams(vmem_limit_bytes=24 * 2**20),
        cost_estimate=pl.CostEstimate(flops=2**20, bytes_accessed=2 * 2**20, transcendentals=0),
    )(*arrays)


def stats_kernel(own_ref, a_ref, b_ref, c_ref, allowed_ref, logits_ref, stats_ref):
    logits = own_ref[...]
    for ref in (a_ref, b_ref, c_ref):
        part = to_f32(ref[:, :HALF]) * scale_of(ref[:, HALF:])
        logits = logits + jnp.concatenate([part[:8], part[8:]], axis=1)
    logits_ref[...] = logits
    allowed = allowed_ref[...] > 0.5
    top = jnp.max(jnp.where(allowed, logits, -1e30), axis=1, keepdims=True)
    scaled = jnp.where(allowed, jnp.exp(logits - top), 0.0)
    total = jnp.sum(scaled, axis=1, keepdims=True)
    weighted = jnp.sum(jnp.where(allowed, scaled * logits, 0.0), axis=1, keepdims=True)
    lane = lax.broadcasted_iota(jnp.int32, (8, 128), 1)
    tile = jnp.where(lane == 0, top, jnp.where(lane == 1, total, jnp.where(lane == 2, weighted, 0.0)))
    stats_ref[...] = jnp.broadcast_to(tile[None], stats_ref.shape)


def finish_kernel(logits_ref, allowed_ref, stats_ref, log_probs_ref, entropy_ref):
    stats = stats_ref[...]
    top = stats[:, :, 0:1]
    row_max = jnp.max(top, axis=0)
    factor = jnp.exp(top - row_max[None])
    total = jnp.sum(stats[:, :, 1:2] * factor, axis=0)
    weighted = jnp.sum(stats[:, :, 2:3] * factor, axis=0)
    log_norm = row_max + jnp.log(total)
    log_probs_ref[...] = jnp.where(allowed_ref[...] > 0.5, logits_ref[...] - log_norm, 0.0)
    entropy_ref[...] = jnp.broadcast_to(log_norm - weighted / total, entropy_ref.shape)


def spread(array, axis):
    return lax.all_to_all(array, axis, 0, 0)


def shift(array, step):
    count = lax.axis_size("rows")
    return lax.ppermute(array, "rows", [(i, (i + step) % count) for i in range(count)])


def shards(hidden_held, head_weight, state_table, row_states, owner):
    z = lax.axis_index("rows").astype(jnp.int32)[None]
    chunks = hidden_held[0, 0].reshape(8, 16, 4, 128).transpose(2, 0, 1, 3).reshape(32, 16, 128)
    mine = lax.dynamic_index_in_dim(spread(chunks, "vocab"), owner[0], 0, keepdims=True)
    x = spread(jnp.broadcast_to(mine, (32, 16, 128)), "vocab")

    own, up, down, up2, down2 = product(z, x, head_weight)
    own, up, far, down = first_sum(own, shift(up, 1), shift(down, -1), shift(up2, 2), shift(down2, -2))

    words = state_table[row_states[0]]
    bits = jnp.right_shift(words[:, :, None], jnp.arange(32, dtype=jnp.int32)) & 1
    allowed = bits.astype(F32).reshape(8, N)

    parts = (shift(up, 4), shift(far, 8), shift(down, -4))
    logits, stats = pl.pallas_call(
        stats_kernel,
        out_shape=[jax.ShapeDtypeStruct((8, N), F32), jax.ShapeDtypeStruct((32, 8, 128), F32)],
    )(own, *parts, allowed)
    stats = spread(stats, "vocab")
    log_probs, entropy = pl.pallas_call(
        finish_kernel,
        out_shape=[jax.ShapeDtypeStruct((8, N), F32), jax.ShapeDtypeStruct((8, 128), F32)],
    )(logits, allowed, stats)
    return log_probs[None], entropy[:, 0][None]


def solution(mesh):
    return jax.shard_map(
        shards,
        mesh=mesh,
        in_specs=(
            P("vocab", None, None, "rows"),
            P("rows", "vocab"),
            P(None, "vocab"),
            P(None, "rows"),
            P(),
        ),
        out_specs=(P(None, "rows", "vocab"), P(None, "rows")),
        check_vma=False,
    )
```

time: 433 us -> 108 us (0.25)
  waiting for transfers between devices: 272 us -> 23.1 us
  blocking collectives: 134 us -> 15.4 us
  starting transfers between devices: 0.08 us -> 51.8 us
  between operations: 14.7 us -> 1.46 us
  Pallas kernels: 0 us -> 7.09 us
  local copies, waits for them, and re-layouts: 1.51 us -> 7.5 us
  matrix products: 5.57 us -> 0 us
    psum x2 -> x0, waiting for transfers between devices: 272 us -> none  [the longest x1 139 us: broadcast(): return lax.psum(kept, axis)]
    pmax x1 -> x0, blocking collectives: 71.6 us -> none  [shards(): row_max = lax.pmax(local_max, 'vocab')]
    psum x1 -> x0, blocking collectives: 62.7 us -> none  [shards(): total, weighted = lax.psum((local_total, local_weighted), 'vocab')]
    ppermute x0 -> x7, starting transfers between devices: none -> 37.5 us  [shift(): lax.ppermute(array, 'rows', [(i, (i + step) % count) for i in range(count)])]
    all_to_all x0 -> x1, blocking collectives: none -> 15.4 us  [spread(): return lax.all_to_all(array, axis, 0, 0)]
    all_to_all x0 -> x2, waiting for transfers between devices: none -> 15 us  [spread(): return lax.all_to_all(array, axis, 0, 0)]
    all_to_all x0 -> x2, starting transfers between devices: none -> 14.3 us  [spread(): return lax.all_to_all(array, axis, 0, 0)]
    ppermute x0 -> x7, waiting for transfers between devices: none -> 8.17 us  [shift(): lax.ppermute(array, 'rows', [(i, (i + step) % count) for i in range(count)])]
  transfers between devices with their start and end apart: 2 -> 9, of which waited for: 2 -> 6; matrix products, arithmetic and copies ran while one was open for 0% -> 2% of each run, Pallas kernels for 0% -> 0%
where the time goes in v1:
time: 108 us; the launch traced here: 107 us
  starting transfers between devices  51.8 us (48%)
  waiting for transfers between devices  23.1 us (21%)
  blocking collectives  15.4 us (14%)
  local copies, waits for them, and re-layouts  7.5 us (7%)
  Pallas kernels  7.09 us (7%)
  between operations  1.46 us (1%)
    ppermute x7, starting transfers between devices, shift(): lax.ppermute(array, 'rows', [(i, (i + step) % count) for i in range(count)])  37.5 us
    all_to_all x1, blocking collectives, spread(): return lax.all_to_all(array, axis, 0, 0)  15.4 us
    all_to_all x2, waiting for transfers between devices, spread(): return lax.all_to_all(array, axis, 0, 0)  15 us
    all_to_all x2, starting transfers between devices, spread(): return lax.all_to_all(array, axis, 0, 0)  14.3 us
    ppermute x7, waiting for transfers between devices, shift(): lax.ppermute(array, 'rows', [(i, (i + step) % count) for i in range(count)])  8.17 us
    unnamed x14, local copies, waits for them, and re-layouts  2.82 us
    pallas_call x1, Pallas kernels, product(): pl.pallas_call(product_kernel, grid=(TILES,), in_specs=[pl.BlockSpec(memo...  2.71 us
  transfers between devices with their start and end apart: 9, of which 6 were waited for; matrix products, arithmetic and copies ran while one was open for 2% of the time, Pallas kernels for 0%

profile of v1, /device:TPU:1, one launch (start us, length us, event | category | flops | bytes accessed | tf_op | source)
XLA Modules:
  0.0 107.1 jit_solution(4807283775604418053)
XLA Ops:
  0.6 0.0 copy-start
  0.6 0.0 copy-start.6
  0.7 1.0 reshape_squeeze.3
  1.6 0.7 copy.7
  2.3 10.4 %all-to-all-start = ((bf16[32,16,128]{2,1,0:T(8,128)(2,1)}), bf16[32,16,128]{2,1,0:T(8,128)(2,1)S(1)}, u32[]{:S(2)}, u32[]{:S(2)}) async-start(bf16[32,16,128]{2,1,0:T(8,128)(2,1)} %bitcast.2), calls=%async_computation | async-start | bytes 262144 | tf_op jit(solution)/shard_map/all_to_all | solution.py:148
  13.3 7.2 %all-to-all-done = bf16[32,16,128]{2,1,0:T(8,128)(2,1)S(1)} async-done(((bf16[32,16,128]{2,1,0:T(8,128)(2,1)}), bf16[32,16,128]{2,1,0:T(8,128)(2,1)S(1)}, u32[]{:S(2)}, u32[]{:S(2)}) %all-to-all-start) | async-done | bytes 131104 | tf_op jit(solution)/shard_map/all_to_all | solution.py:148
  20.5 0.7 broadcast_in_dim.18
  21.2 3.9 %all-to-all-start.1 = ((bf16[32,16,128]{2,1,0:T(8,128)(2,1)}), bf16[32,16,128]{2,1,0:T(8,128)(2,1)S(1)}, u32[]{:S(2)}, u32[]{:S(2)}) async-start(bf16[32,16,128]{2,1,0:T(8,128)(2,1)} %broadcast_in_dim.18), calls=%async_computation.1 | async-start | bytes 262144 | tf_op jit(solution)/shard_map/all_to_all | solution.py:148
  25.1 7.8 %all-to-all-done.1.x_ref = bf16[32,16,128]{2,1,0:T(8,128)(2,1)S(1)} async-done(((bf16[32,16,128]{2,1,0:T(8,128)(2,1)}), bf16[32,16,128]{2,1,0:T(8,128)(2,1)S(1)}, u32[]{:S(2)}, u32[]{:S(2)}) %all-to-all-start.1) | async-done | bytes 131104 | tf_op jit(solution)/shard_map/all_to_all | solution.py:148
  32.9 0.0 copy-start.1
  32.9 2.2 %copy-done.1 = bf16[512,4096]{1,0:T(8,128)(2,1)S(1)} copy-done((bf16[512,4096]{1,0:T(8,128)(2,1)S(1)}, bf16[512,4096]{1,0:T(8,128)(2,1)}, u32[]{:S(2)}) %copy-start.1) | copy-done | bytes 4194328
  35.1 2.7 %shard_map.68 = (f32[32,4096]{1,0:T(8,128)S(1)}, s16[32,4224]{1,0:T(8,128)(2,1)S(1)}, s16[32,4224]{1,0:T(8,128)(2,1)S(1)}, s16[32,2176]{1,0:T(8,128)(2,1)S(1)}, s16[32,2176]{1,0:T(8,128)(2,1)S(1)}) custom-call(s32[1]{0:T(128)} %bitcast.z_ref, bf16[32,16,128]{2,1,0:T(8,128)(2,1)S(1)} %all-to-all-done.1.x_ref, bf16[512,4096]{1,0:T(8,128)(2,1)S(1)} %copy-done.1), custom_call_target="tpu_custom_call" | custom-call | flops 536870912 | bytes 6291456 | tf_op jit(solution)/shard_map/pallas_call | solution.py:73
  37.8 1.9 %collective-permute-start = (s16[32,4224]{1,0:T(8,128)(2,1)S(1)}, s16[32,4224]{1,0:T(8,128)(2,1)S(1)}, u32[]{:S(2)}, u32[]{:S(2)}) collective-permute-start(s16[32,4224]{1,0:T(8,128)(2,1)S(1)} %get-tuple-element.16), channel_id=1, source_target_pairs={{0,32},{32,64},{64,96},{96,128},{128,160},{160,192},{192,224},{224... | collective-permute-start | bytes 811016 | tf_op jit(solution)/shard_map/ppermute | solution.py:153
  39.7 9.2 %collective-permute-start.1 = (s16[32,4224]{1,0:T(8,128)(2,1)S(1)}, s16[32,4224]{1,0:T(8,128)(2,1)S(1)}, u32[]{:S(2)}, u32[]{:S(2)}) collective-permute-start(s16[32,4224]{1,0:T(8,128)(2,1)S(1)} %get-tuple-element.17), channel_id=1, source_target_pairs={{0,480},{32,0},{64,32},{96,64},{128,96},{160,128},{192,160},{224,1... | collective-permute-start | bytes 811016 | tf_op jit(solution)/shard_map/ppermute | solution.py:153
  49.0 1.9 %collective-permute-start.2 = (s16[32,2176]{1,0:T(8,128)(2,1)S(1)}, s16[32,2176]{1,0:T(8,128)(2,1)S(1)}, u32[]{:S(2)}, u32[]{:S(2)}) collective-permute-start(s16[32,2176]{1,0:T(8,128)(2,1)S(1)} %get-tuple-element.18), channel_id=1, source_target_pairs={{0,64},{32,96},{64,128},{96,160},{128,192},{160,224},{192,256},{22... | collective-permute-start | bytes 417800 | tf_op jit(solution)/shard_map/ppermute | solution.py:153
  50.9 5.5 %collective-permute-start.3 = (s16[32,2176]{1,0:T(8,128)(2,1)S(1)}, s16[32,2176]{1,0:T(8,128)(2,1)S(1)}, u32[]{:S(2)}, u32[]{:S(2)}) collective-permute-start(s16[32,2176]{1,0:T(8,128)(2,1)S(1)} %get-tuple-element.19), channel_id=1, source_target_pairs={{0,448},{32,480},{64,0},{96,32},{128,64},{160,96},{192,128},{224,1... | collective-permute-start | bytes 417800 | tf_op jit(solution)/shard_map/ppermute | solution.py:153
  56.4 0.0 copy-done.6
  56.4 0.0 copy-done
  56.4 0.6 gather_fusion
  57.0 0.2 shift_right_arithmetic.20
  57.2 0.2 shift_right_arithmetic.21
  57.4 0.1 shift_right_arithmetic.23
  57.5 2.9 %collective-permute-done.2.low2_ref = s16[32,2176]{1,0:T(8,128)(2,1)S(1)} collective-permute-done((s16[32,2176]{1,0:T(8,128)(2,1)S(1)}, s16[32,2176]{1,0:T(8,128)(2,1)S(1)}, u32[]{:S(2)}, u32[]{:S(2)}) %collective-permute-start.2) | collective-permute-done | bytes 139296 | tf_op jit(solution)/shard_map/ppermute | solution.py:153
  60.4 0.6 collective-permute-done.3.high2_ref
  60.9 0.0 collective-permute-done.low_ref
  60.9 0.0 collective-permute-done.1.high_ref
  60.9 0.4 shard_map.69
  61.3 0.0 copy-start.2
  61.3 8.1 %collective-permute-start.4 = (s16[16,2176]{1,0:T(8,128)(2,1)S(1)}, s16[16,2176]{1,0:T(8,128)(2,1)S(1)}, u32[]{:S(2)}, u32[]{:S(2)}) collective-permute-start(s16[16,2176]{1,0:T(8,128)(2,1)S(1)} %get-tuple-element.21), channel_id=1, source_target_pairs={{0,128},{32,160},{64,192},{96,224},{128,256},{160,288},{192,320},{... | collective-permute-start | bytes 208904 | tf_op jit(solution)/shard_map/ppermute | solution.py:153
  69.4 5.0 %collective-permute-start.5 = (s16[16,2176]{1,0:T(8,128)(2,1)S(1)}, s16[16,2176]{1,0:T(8,128)(2,1)S(1)}, u32[]{:S(2)}, u32[]{:S(2)}) collective-permute-start(s16[16,2176]{1,0:T(8,128)(2,1)S(1)} %get-tuple-element.22), channel_id=1, source_target_pairs={{0,256},{32,288},{64,320},{96,352},{128,384},{160,416},{192,448},{... | collective-permute-start | bytes 208904 | tf_op jit(solution)/shard_map/ppermute | solution.py:153
  74.4 5.9 %collective-permute-start.6 = (s16[16,2176]{1,0:T(8,128)(2,1)S(1)}, s16[16,2176]{1,0:T(8,128)(2,1)S(1)}, u32[]{:S(2)}, u32[]{:S(2)}) collective-permute-start(s16[16,2176]{1,0:T(8,128)(2,1)S(1)} %get-tuple-element.23), channel_id=1, source_target_pairs={{0,384},{32,416},{64,448},{96,480},{128,0},{160,32},{192,64},{224,... | collective-permute-start | bytes 208904 | tf_op jit(solution)/shard_map/ppermute | solution.py:153
  80.3 0.7 and_convert_fusion.allowed_ref
  81.0 0.0 collective-permute-done.4.a_ref
  81.0 0.0 copy-start.3
  81.0 2.7 %collective-permute-done.5.b_ref = s16[16,2176]{1,0:T(8,128)(2,1)S(1)} collective-permute-done((s16[16,2176]{1,0:T(8,128)(2,1)S(1)}, s16[16,2176]{1,0:T(8,128)(2,1)S(1)}, u32[]{:S(2)}, u32[]{:S(2)}) %collective-permute-start.5) | collective-permute-done | bytes 69664 | tf_op jit(solution)/shard_map/ppermute | solution.py:153
  83.7 0.0 copy-start.4
  83.7 2.1 %collective-permute-done.6.c_ref = s16[16,2176]{1,0:T(8,128)(2,1)S(1)} collective-permute-done((s16[16,2176]{1,0:T(8,128)(2,1)S(1)}, s16[16,2176]{1,0:T(8,128)(2,1)S(1)}, u32[]{:S(2)}, u32[]{:S(2)}) %collective-permute-start.6) | collective-permute-done | bytes 69664 | tf_op jit(solution)/shard_map/ppermute | solution.py:153
  85.8 0.0 copy-start.5
  85.8 0.0 copy-done.2
  85.8 0.0 copy-done.3
  85.8 0.0 copy-done.4
  85.8 0.6 copy-done.5
  86.4 2.0 %shard_map.70 = (f32[8,4096]{1,0:T(8,128)}, f32[32,8,128]{2,1,0:T(8,128)}) custom-call(f32[8,4096]{1,0:T(8,128)} %copy-done.2, s16[16,2176]{1,0:T(8,128)(2,1)} %copy-done.3, s16[16,2176]{1,0:T(8,128)(2,1)} %copy-done.4, s16[16,2176]{1,0:T(8,128)(2,1)} %copy-done.5, f32[8,4096]{1,0:T(8,128)} %and_convert_fusion.allowed_ref), custom_call_target="tpu_custom_call" | custom-call | tf_op jit(solution)/shard_map/pallas_call | solution.py:170
  88.4 15.4 %all_to_all.15.stats_ref = f32[32,8,128]{2,1,0:T(8,128)} all-to-all(f32[32,8,128]{2,1,0:T(8,128)} %get-tuple-element.25), channel_id=1, replica_groups=mesh['rows'=16,'vocab'=32] {'vocab'}, dimensions={0} | all-to-all | bytes 262144 | tf_op jit(solution)/shard_map/all_to_all | solution.py:148
  103.8 2.0 %shard_map.71 = (f32[8,4096]{1,0:T(8,128)}, f32[8,128]{1,0:T(8,128)}) custom-call(f32[8,4096]{1,0:T(8,128)} %get-tuple-element.24.logits_ref, f32[8,4096]{1,0:T(8,128)} %and_convert_fusion.allowed_ref, f32[32,8,128]{2,1,0:T(8,128)} %all_to_all.15.stats_ref), custom_call_target="tpu_custom_call" | custom-call | tf_op jit(solution)/shard_map/pallas_call | solution.py:175
  105.8 1.3 %slice_reduce_fusion = f32[8]{0:T(128)} fusion(f32[8,128]{1,0:T(8,128)} %get-tuple-element.27), kind=kLoop, calls=%fused_computation.3 | loop fusion | bytes 64 | tf_op jit(solution)/shard_map/slice | solution.py:179
  (4 shorter events, 0.0 us)
Async XLA Ops:
  0.6 55.8 %copy-start = (s32[24,128]{1,0:T(8,128)S(1)}, s32[24,128]{1,0:T(8,128)}, u32[]{:S(2)}) copy-start(s32[24,128]{1,0:T(8,128)} %param.7) | copy-start | bytes 36868
  0.6 55.7 %copy-start.6 = (s32[1,8]{1,0:T(1,128)S(1)}, s32[1,8]{1,0:T(1,128)}, u32[]{:S(2)}) copy-start(s32[1,8]{1,0:T(1,128)} %param.8) | copy-start | bytes 100
  2.3 18.2 %all-to-all-start = ((bf16[32,16,128]{2,1,0:T(8,128)(2,1)}), bf16[32,16,128]{2,1,0:T(8,128)(2,1)S(1)}, u32[]{:S(2)}, u32[]{:S(2)}) async-start(bf16[32,16,128]{2,1,0:T(8,128)(2,1)} %bitcast.2), calls=%async_computation | async-start | bytes 262144 | tf_op jit(solution)/shard_map/all_to_all | solution.py:148
  21.2 11.7 %all-to-all-start.1 = ((bf16[32,16,128]{2,1,0:T(8,128)(2,1)}), bf16[32,16,128]{2,1,0:T(8,128)(2,1)S(1)}, u32[]{:S(2)}, u32[]{:S(2)}) async-start(bf16[32,16,128]{2,1,0:T(8,128)(2,1)} %broadcast_in_dim.18), calls=%async_computation.1 | async-start | bytes 262144 | tf_op jit(solution)/shard_map/all_to_all | solution.py:148
  32.9 2.2 %copy-start.1 = (bf16[512,4096]{1,0:T(8,128)(2,1)S(1)}, bf16[512,4096]{1,0:T(8,128)(2,1)}, u32[]{:S(2)}) copy-start(bf16[512,4096]{1,0:T(8,128)(2,1)} %w_ref.1) | copy-start | bytes 12582916
  37.8 23.1 %collective-permute-start = (s16[32,4224]{1,0:T(8,128)(2,1)S(1)}, s16[32,4224]{1,0:T(8,128)(2,1)S(1)}, u32[]{:S(2)}, u32[]{:S(2)}) collective-permute-start(s16[32,4224]{1,0:T(8,128)(2,1)S(1)} %get-tuple-element.16), channel_id=1, source_target_pairs={{0,32},{32,64},{64,96},{96,128},{128,160},{160,192},{192,224},{224... | collective-permute-start | bytes 811016 | tf_op jit(solution)/shard_map/ppermute | solution.py:153
  39.7 21.2 %collective-permute-start.1 = (s16[32,4224]{1,0:T(8,128)(2,1)S(1)}, s16[32,4224]{1,0:T(8,128)(2,1)S(1)}, u32[]{:S(2)}, u32[]{:S(2)}) collective-permute-start(s16[32,4224]{1,0:T(8,128)(2,1)S(1)} %get-tuple-element.17), channel_id=1, source_target_pairs={{0,480},{32,0},{64,32},{96,64},{128,96},{160,128},{192,160},{224,1... | collective-permute-start | bytes 811016 | tf_op jit(solution)/shard_map/ppermute | solution.py:153
  49.0 11.4 %collective-permute-start.2 = (s16[32,2176]{1,0:T(8,128)(2,1)S(1)}, s16[32,2176]{1,0:T(8,128)(2,1)S(1)}, u32[]{:S(2)}, u32[]{:S(2)}) collective-permute-start(s16[32,2176]{1,0:T(8,128)(2,1)S(1)} %get-tuple-element.18), channel_id=1, source_target_pairs={{0,64},{32,96},{64,128},{96,160},{128,192},{160,224},{192,256},{22... | collective-permute-start | bytes 417800 | tf_op jit(solution)/shard_map/ppermute | solution.py:153
  50.9 10.0 %collective-permute-start.3 = (s16[32,2176]{1,0:T(8,128)(2,1)S(1)}, s16[32,2176]{1,0:T(8,128)(2,1)S(1)}, u32[]{:S(2)}, u32[]{:S(2)}) collective-permute-start(s16[32,2176]{1,0:T(8,128)(2,1)S(1)} %get-tuple-element.19), channel_id=1, source_target_pairs={{0,448},{32,480},{64,0},{96,32},{128,64},{160,96},{192,128},{224,1... | collective-permute-start | bytes 417800 | tf_op jit(solution)/shard_map/ppermute | solution.py:153
  61.3 24.5 %copy-start.2 = (f32[8,4096]{1,0:T(8,128)}, f32[8,4096]{1,0:T(8,128)S(1)}, u32[]{:S(2)}) copy-start(f32[8,4096]{1,0:T(8,128)S(1)} %get-tuple-element.20.own_ref) | copy-start | bytes 393220
  61.3 19.7 %collective-permute-start.4 = (s16[16,2176]{1,0:T(8,128)(2,1)S(1)}, s16[16,2176]{1,0:T(8,128)(2,1)S(1)}, u32[]{:S(2)}, u32[]{:S(2)}) collective-permute-start(s16[16,2176]{1,0:T(8,128)(2,1)S(1)} %get-tuple-element.21), channel_id=1, source_target_pairs={{0,128},{32,160},{64,192},{96,224},{128,256},{160,288},{192,320},{... | collective-permute-start | bytes 208904 | tf_op jit(solution)/shard_map/ppermute | solution.py:153
  69.4 14.2 %collective-permute-start.5 = (s16[16,2176]{1,0:T(8,128)(2,1)S(1)}, s16[16,2176]{1,0:T(8,128)(2,1)S(1)}, u32[]{:S(2)}, u32[]{:S(2)}) collective-permute-start(s16[16,2176]{1,0:T(8,128)(2,1)S(1)} %get-tuple-element.22), channel_id=1, source_target_pairs={{0,256},{32,288},{64,320},{96,352},{128,384},{160,416},{192,448},{... | collective-permute-start | bytes 208904 | tf_op jit(solution)/shard_map/ppermute | solution.py:153
  74.4 11.3 %collective-permute-start.6 = (s16[16,2176]{1,0:T(8,128)(2,1)S(1)}, s16[16,2176]{1,0:T(8,128)(2,1)S(1)}, u32[]{:S(2)}, u32[]{:S(2)}) collective-permute-start(s16[16,2176]{1,0:T(8,128)(2,1)S(1)} %get-tuple-element.23), channel_id=1, source_target_pairs={{0,384},{32,416},{64,448},{96,480},{128,0},{160,32},{192,64},{224,... | collective-permute-start | bytes 208904 | tf_op jit(solution)/shard_map/ppermute | solution.py:153
  81.0 4.8 %copy-start.3 = (s16[16,2176]{1,0:T(8,128)(2,1)}, s16[16,2176]{1,0:T(8,128)(2,1)S(1)}, u32[]{:S(2)}) copy-start(s16[16,2176]{1,0:T(8,128)(2,1)S(1)} %collective-permute-done.4.a_ref) | copy-start | bytes 208900
  83.7 2.1 %copy-start.4 = (s16[16,2176]{1,0:T(8,128)(2,1)}, s16[16,2176]{1,0:T(8,128)(2,1)S(1)}, u32[]{:S(2)}) copy-start(s16[16,2176]{1,0:T(8,128)(2,1)S(1)} %collective-permute-done.5.b_ref) | copy-start | bytes 208900
  85.8 0.6 copy-start.5

commit v2 on v1

v2 whole, which is shorter than its diff:
```python
import jax
import jax.numpy as jnp
from jax import lax
from jax.experimental import pallas as pl
from jax.experimental.pallas import tpu as pltpu
from jax.sharding import PartitionSpec as P

N = 4096
HALF = N // 2
TAIL = 128
TILES = 8
WIDE = N // TILES
F32 = jnp.float32
I16 = jnp.int16


def encode(values):
    top = jnp.max(jnp.abs(values), axis=1, keepdims=True)
    k = jnp.ceil(8.0 * jnp.log2(jnp.maximum(top, 1e-30) * (1.0 / 32000.0)))
    return jnp.round(values * jnp.exp2(-0.125 * k)), k


def to_i16(values):
    return values.astype(jnp.int32).astype(I16)


def to_f32(codes):
    return codes.astype(jnp.int32).astype(F32)


def scale_of(codes):
    return jnp.exp2(0.125 * to_f32(codes)[:, :1])


def product_kernel(z_ref, x_ref, w_ref, own_ref, up_ref, down_ref, up2_ref, down2_ref, acc_ref, held_ref, sems):
    def tile(t):
        part = pl.ds(t * WIDE, WIDE)
        return pltpu.make_async_copy(w_ref.at[:, part], held_ref.at[:, part], sems.at[t])

    for t in range(TILES):
        tile(t).start()
    x = x_ref[...].astype(F32).reshape(16, 2, 2, 8, 128)
    x = [x[:, h, t].reshape(128, 128) for h in range(2) for t in range(2)]
    x = jnp.concatenate(x, axis=1).astype(jnp.bfloat16)
    i = lax.broadcasted_iota(jnp.int32, (128, 128), 0)
    source = lax.broadcasted_iota(jnp.int32, (128, 128), 1)
    b = i >> 5
    piece = (z_ref[0] + jnp.where(b == 3, -1, b) + 4 * ((i >> 3) & 3)) & 15
    chosen = (source == 8 * piece + (i & 7)).astype(F32).astype(jnp.bfloat16)
    x = jnp.dot(chosen, x, preferred_element_type=F32).astype(jnp.bfloat16)
    for t in range(TILES):
        tile(t).wait()
        acc_ref[:, t * WIDE : (t + 1) * WIDE] = jnp.dot(
            x, held_ref[:, t * WIDE : (t + 1) * WIDE], preferred_element_type=F32
        )
    own_ref[...] = acc_ref[:32]
    for ref, lo in ((up_ref, 32), (down_ref, 96)):
        q, k = encode(acc_ref[lo : lo + 32])
        ref[:, :N] = to_i16(q)
        ref[:, N:] = to_i16(jnp.broadcast_to(k, (32, TAIL)))
    q, k = encode(acc_ref[64:96])
    tail = to_i16(jnp.broadcast_to(k, (32, TAIL)))
    up2_ref[:, :HALF] = to_i16(q[:, :HALF])
    up2_ref[:, HALF:] = tail
    down2_ref[:, :HALF] = to_i16(q[:, HALF:])
    down2_ref[:, HALF:] = tail


def product(z, x, w):
    outs = ((32, N), (32, N + TAIL), (32, N + TAIL), (32, HALF + TAIL), (32, HALF + TAIL))
    return pl.pallas_call(
        product_kernel,
        in_specs=[
            pl.BlockSpec(memory_space=pltpu.SMEM),
            pl.BlockSpec(memory_space=pltpu.VMEM),
            pl.BlockSpec(memory_space=pl.ANY),
        ],
        out_shape=[jax.ShapeDtypeStruct(s, F32 if n == 0 else I16) for n, s in enumerate(outs)],
        scratch_shapes=[
            pltpu.VMEM((128, N), F32),
            pltpu.VMEM(w.shape, w.dtype),
            pltpu.SemaphoreType.DMA((TILES,)),
        ],
        compiler_params=pltpu.CompilerParams(vmem_limit_bytes=50 * 2**20),
        cost_estimate=pl.CostEstimate(flops=2 * 128 * 512 * N, bytes_accessed=6 * 2**20, transcendentals=0),
    )(z, x, w)


def first_sum_kernel(own_ref, low_ref, high_ref, low2_ref, high2_ref, keep_ref, up_ref, far_ref, down_ref):
    near = (
        own_ref[...]
        + to_f32(low_ref[:, :N]) * scale_of(low_ref[:, N:])
        + to_f32(high_ref[:, :N]) * scale_of(high_ref[:, N:])
    )
    left = to_f32(low2_ref[:, :HALF]) * scale_of(low2_ref[:, HALF:])
    right = to_f32(high2_ref[:, :HALF]) * scale_of(high2_ref[:, HALF:])
    right = jnp.concatenate([right[24:], right[:24]], axis=0)
    total = near + jnp.concatenate([left, right], axis=1)
    keep_ref[...] = total[:8]
    for ref, lo in ((up_ref, 8), (far_ref, 16), (down_ref, 24)):
        q, k = encode(total[lo : lo + 8])
        ref[:, :HALF] = to_i16(jnp.concatenate([q[:, :HALF], q[:, HALF:]], axis=0))
        ref[:, HALF:] = to_i16(jnp.broadcast_to(jnp.concatenate([k, k], axis=0), (16, TAIL)))


def first_sum(*arrays):
    coded = jax.ShapeDtypeStruct((16, HALF + TAIL), I16)
    return pl.pallas_call(
        first_sum_kernel,
        out_shape=[jax.ShapeDtypeStruct((8, N), F32), coded, coded, coded],
        compiler_params=pltpu.CompilerParams(vmem_limit_bytes=24 * 2**20),
        cost_estimate=pl.CostEstimate(flops=2**20, bytes_accessed=2 * 2**20, transcendentals=0),
    )(*arrays)


def stats_kernel(own_ref, a_ref, b_ref, c_ref, allowed_ref, logits_ref, stats_ref):
    logits = own_ref[...]
    for ref in (a_ref, b_ref, c_ref):
        part = to_f32(ref[:, :HALF]) * scale_of(ref[:, HALF:])
        logits = logits + jnp.concatenate([part[:8], part[8:]], axis=1)
    logits_ref[...] = logits
    allowed = allowed_ref[...] > 0.5
    top = jnp.max(jnp.where(allowed, logits, -1e30), axis=1, keepdims=True)
    scaled = jnp.where(allowed, jnp.exp(logits - top), 0.0)
    total = jnp.sum(scaled, axis=1, keepdims=True)
    weighted = jnp.sum(jnp.where(allowed, scaled * logits, 0.0), axis=1, keepdims=True)
    own_lane = lax.broadcasted_iota(jnp.int32, (8, 128), 1) == lax.broadcasted_iota(jnp.int32, (8, 128), 0)
    for n, column in enumerate((top, total, weighted)):
        row = jnp.sum(jnp.where(own_lane, column, 0.0), axis=0, keepdims=True)
        stats_ref[:, :, 128 * n : 128 * n + 128] = jnp.broadcast_to(row[None], (32, 1, 128))


def finish_kernel(logits_ref, allowed_ref, stats_ref, log_probs_ref, entropy_ref):
    top = stats_ref[:, :, :128]
    row_max = jnp.max(top, axis=0)
    factor = jnp.exp(top - row_max[None])
    lane = lax.broadcasted_iota(jnp.int32, (1, 128), 1)
    total = jnp.where(lane < 8, jnp.sum(stats_ref[:, :, 128:256] * factor, axis=0), 1.0)
    weighted = jnp.sum(stats_ref[:, :, 256:] * factor, axis=0)
    log_norm = row_max + jnp.log(total)
    entropy_ref[...] = (log_norm - weighted / total)[:, :8]
    own_lane = lax.broadcasted_iota(jnp.int32, (8, 128), 1) == lax.broadcasted_iota(jnp.int32, (8, 128), 0)
    column = jnp.sum(jnp.where(own_lane, log_norm, 0.0), axis=1, keepdims=True)
    log_probs_ref[0] = jnp.where(allowed_ref[...] > 0.5, logits_ref[...] - column, 0.0)


def spread(array, axis):
    return lax.all_to_all(array, axis, 0, 0)


def shift(array, step):
    count = lax.axis_size("rows")
    return lax.ppermute(array, "rows", [(i, (i + step) % count) for i in range(count)])


def shards(hidden_held, head_weight, state_table, row_states, owner):
    z = lax.axis_index("rows").astype(jnp.int32)[None]
    chunks = hidden_held[0, 0].reshape(16, 8, 4, 128).transpose(0, 2, 1, 3).reshape(32, 16, 128)
    mine = lax.dynamic_index_in_dim(spread(chunks, "vocab"), owner[0], 0, keepdims=True)
    x = spread(jnp.broadcast_to(mine, (32, 16, 128)), "vocab")

    own, up, down, up2, down2 = product(z, x, head_weight)
    low2, low, high, high2 = shift(up2, 2), shift(up, 1), shift(down, -1), shift(down2, -2)
    own, up, far, down = first_sum(own, low, high, low2, high2)

    words = state_table[row_states[0]]
    bits = jnp.right_shift(words[:, :, None], jnp.arange(32, dtype=jnp.int32)) & 1
    allowed = bits.astype(F32).reshape(8, N)

    parts = (shift(far, 8), shift(up, 4), shift(down, -4))
    logits, stats = pl.pallas_call(
        stats_kernel,
        out_shape=[jax.ShapeDtypeStruct((8, N), F32), jax.ShapeDtypeStruct((32, 1, 384), F32)],
        compiler_params=pltpu.CompilerParams(vmem_limit_bytes=24 * 2**20),
    )(own, *parts, allowed)
    stats = spread(stats, "vocab")
    return tuple(
        pl.pallas_call(
            finish_kernel,
            out_shape=[jax.ShapeDtypeStruct((1, 8, N), F32), jax.ShapeDtypeStruct((1, 8), F32)],
            compiler_params=pltpu.CompilerParams(vmem_limit_bytes=24 * 2**20),
        )(logits, allowed, stats)
    )


def solution(mesh):
    return jax.shard_map(
        shards,
        mesh=mesh,
        in_specs=(
            P("vocab", None, None, "rows"),
            P("rows", "vocab"),
            P(None, "vocab"),
            P(None, "rows"),
            P(),
        ),
        out_specs=(P(None, "rows", "vocab"), P(None, "rows")),
        check_vma=False,
    )
```

time: 108 us -> 96.3 us (0.89)
  local copies, waits for them, and re-layouts: 7.5 us -> 1.76 us
  blocking collectives: 15.4 us -> 12.1 us
  Pallas kernels: 7.09 us -> 4.8 us
    all_to_all x1, blocking collectives: 15.4 us -> 12.1 us  [spread(): return lax.all_to_all(array, axis, 0, 0)]
    unnamed x14 -> x4, local copies, waits for them, and re-layouts: 2.82 us -> 0.01 us
    pallas_call x1, Pallas kernels: 2.05 us -> 0.35 us  [shards(): pl.pallas_call(stats_kernel, out_shape=[jax.ShapeDtypeStruct((8, N), F32)...]
    slice x1 -> x0, local copies, waits for them, and re-layouts: 1.31 us -> none  [shards(): return (log_probs[None], entropy[:, 0][None])]
  transfers between devices with their start and end apart: 9 -> 9, of which waited for: 6 -> 6; matrix products, arithmetic and copies ran while one was open for 2% -> 1% of each run, Pallas kernels for 0% -> 0%
where the time goes in v2:
time: 96.3 us; the launch traced here: 95 us
  starting transfers between devices  52 us (54%)
  waiting for transfers between devices  22.9 us (24%)
  blocking collectives  12.1 us (13%)
  Pallas kernels  4.8 us (5%)
  local copies, waits for them, and re-layouts  1.76 us (2%)
  between operations  1.46 us (2%)
    ppermute x7, starting transfers between devices, shift(): lax.ppermute(array, 'rows', [(i, (i + step) % count) for i in range(count)])  37.5 us
    all_to_all x2, waiting for transfers between devices, spread(): return lax.all_to_all(array, axis, 0, 0)  15 us
    all_to_all x2, starting transfers between devices, spread(): return lax.all_to_all(array, axis, 0, 0)  14.4 us
    all_to_all x1, blocking collectives, spread(): return lax.all_to_all(array, axis, 0, 0)  12.1 us
    ppermute x7, waiting for transfers between devices, shift(): lax.ppermute(array, 'rows', [(i, (i + step) % count) for i in range(count)])  7.93 us
    pallas_call x1, Pallas kernels, product(): pl.pallas_call(product_kernel, in_specs=[pl.BlockSpec(memory_space=pltpu....  3.26 us
  transfers between devices with their start and end apart: 9, of which 6 were waited for; matrix products, arithmetic and copies ran while one was open for 1% of the time, Pallas kernels for 0%

profile of v2, /device:TPU:1, one launch (start us, length us, event | category | flops | bytes accessed | tf_op | source)
XLA Modules:
  0.0 95.0 jit_solution(12189990347493978003)
XLA Ops:
  0.6 0.0 copy-start
  0.6 0.0 copy-start.1
  0.7 10.5 %all-to-all-start = ((bf16[32,16,128]{2,1,0:T(8,128)(2,1)}), bf16[32,16,128]{2,1,0:T(8,128)(2,1)S(1)}, u32[]{:S(2)}, u32[]{:S(2)}) async-start(bf16[32,16,128]{2,1,0:T(8,128)(2,1)} %bitcast.16), calls=%async_computation | async-start | bytes 262144 | tf_op jit(solution)/shard_map/all_to_all | solution.py:148
  11.8 7.2 %all-to-all-done = bf16[32,16,128]{2,1,0:T(8,128)(2,1)S(1)} async-done(((bf16[32,16,128]{2,1,0:T(8,128)(2,1)}), bf16[32,16,128]{2,1,0:T(8,128)(2,1)S(1)}, u32[]{:S(2)}, u32[]{:S(2)}) %all-to-all-start) | async-done | bytes 131104 | tf_op jit(solution)/shard_map/all_to_all | solution.py:148
  19.0 0.7 broadcast_in_dim.15
  19.7 3.9 %all-to-all-start.1 = ((bf16[32,16,128]{2,1,0:T(8,128)(2,1)}), bf16[32,16,128]{2,1,0:T(8,128)(2,1)S(1)}, u32[]{:S(2)}, u32[]{:S(2)}) async-start(bf16[32,16,128]{2,1,0:T(8,128)(2,1)} %broadcast_in_dim.15), calls=%async_computation.1 | async-start | bytes 262144 | tf_op jit(solution)/shard_map/all_to_all | solution.py:148
  23.6 7.8 %all-to-all-done.1.x_ref = bf16[32,16,128]{2,1,0:T(8,128)(2,1)S(1)} async-done(((bf16[32,16,128]{2,1,0:T(8,128)(2,1)}), bf16[32,16,128]{2,1,0:T(8,128)(2,1)S(1)}, u32[]{:S(2)}, u32[]{:S(2)}) %all-to-all-start.1) | async-done | bytes 131104 | tf_op jit(solution)/shard_map/all_to_all | solution.py:148
  31.4 3.3 %shard_map.68 = (f32[32,4096]{1,0:T(8,128)S(1)}, s16[32,4224]{1,0:T(8,128)(2,1)S(1)}, s16[32,4224]{1,0:T(8,128)(2,1)S(1)}, s16[32,2176]{1,0:T(8,128)(2,1)S(1)}, s16[32,2176]{1,0:T(8,128)(2,1)S(1)}) custom-call(s32[1]{0:T(128)} %bitcast.z_ref, bf16[32,16,128]{2,1,0:T(8,128)(2,1)S(1)} %all-to-all-done.1.x_ref, bf16[512,4096]{1,0:T(8,128)(2,1)} %w_ref.1), custom_call_target="tpu_custom_call" | custom-call | flops 536870912 | bytes 6291456 | tf_op jit(solution)/shard_map/pallas_call | solution.py:71
  34.7 1.9 %collective-permute-start = (s16[32,4224]{1,0:T(8,128)(2,1)S(1)}, s16[32,4224]{1,0:T(8,128)(2,1)S(1)}, u32[]{:S(2)}, u32[]{:S(2)}) collective-permute-start(s16[32,4224]{1,0:T(8,128)(2,1)S(1)} %get-tuple-element.14), channel_id=1, source_target_pairs={{0,32},{32,64},{64,96},{96,128},{128,160},{160,192},{192,224},{224... | collective-permute-start | bytes 811016 | tf_op jit(solution)/shard_map/ppermute | solution.py:153
  36.6 9.2 %collective-permute-start.1 = (s16[32,4224]{1,0:T(8,128)(2,1)S(1)}, s16[32,4224]{1,0:T(8,128)(2,1)S(1)}, u32[]{:S(2)}, u32[]{:S(2)}) collective-permute-start(s16[32,4224]{1,0:T(8,128)(2,1)S(1)} %get-tuple-element.15), channel_id=1, source_target_pairs={{0,480},{32,0},{64,32},{96,64},{128,96},{160,128},{192,160},{224,1... | collective-permute-start | bytes 811016 | tf_op jit(solution)/shard_map/ppermute | solution.py:153
  45.8 1.9 %collective-permute-start.2 = (s16[32,2176]{1,0:T(8,128)(2,1)S(1)}, s16[32,2176]{1,0:T(8,128)(2,1)S(1)}, u32[]{:S(2)}, u32[]{:S(2)}) collective-permute-start(s16[32,2176]{1,0:T(8,128)(2,1)S(1)} %get-tuple-element.16), channel_id=1, source_target_pairs={{0,64},{32,96},{64,128},{96,160},{128,192},{160,224},{192,256},{22... | collective-permute-start | bytes 417800 | tf_op jit(solution)/shard_map/ppermute | solution.py:153
  47.8 5.5 %collective-permute-start.3 = (s16[32,2176]{1,0:T(8,128)(2,1)S(1)}, s16[32,2176]{1,0:T(8,128)(2,1)S(1)}, u32[]{:S(2)}, u32[]{:S(2)}) collective-permute-start(s16[32,2176]{1,0:T(8,128)(2,1)S(1)} %get-tuple-element.17), channel_id=1, source_target_pairs={{0,448},{32,480},{64,0},{96,32},{128,64},{160,96},{192,128},{224,1... | collective-permute-start | bytes 417800 | tf_op jit(solution)/shard_map/ppermute | solution.py:153
  53.2 0.0 copy-done.1
  53.3 0.0 copy-done
  53.3 0.6 gather_fusion
  53.9 0.2 shift_right_arithmetic.20
  54.0 0.2 shift_right_arithmetic.21
  54.3 0.1 shift_right_arithmetic.23
  54.4 2.9 %collective-permute-done.2.low2_ref = s16[32,2176]{1,0:T(8,128)(2,1)S(1)} collective-permute-done((s16[32,2176]{1,0:T(8,128)(2,1)S(1)}, s16[32,2176]{1,0:T(8,128)(2,1)S(1)}, u32[]{:S(2)}, u32[]{:S(2)}) %collective-permute-start.2) | collective-permute-done | bytes 139296 | tf_op jit(solution)/shard_map/ppermute | solution.py:153
  57.2 0.6 collective-permute-done.3.high2_ref
  57.8 0.0 collective-permute-done.low_ref
  57.8 0.0 collective-permute-done.1.high_ref
  57.8 0.4 shard_map.69
  58.2 9.8 %collective-permute-start.4 = (s16[16,2176]{1,0:T(8,128)(2,1)S(1)}, s16[16,2176]{1,0:T(8,128)(2,1)S(1)}, u32[]{:S(2)}, u32[]{:S(2)}) collective-permute-start(s16[16,2176]{1,0:T(8,128)(2,1)S(1)} %get-tuple-element.19), channel_id=1, source_target_pairs={{0,256},{32,288},{64,320},{96,352},{128,384},{160,416},{192,448},{... | collective-permute-start | bytes 208904 | tf_op jit(solution)/shard_map/ppermute | solution.py:153
  68.0 3.3 %collective-permute-start.5 = (s16[16,2176]{1,0:T(8,128)(2,1)S(1)}, s16[16,2176]{1,0:T(8,128)(2,1)S(1)}, u32[]{:S(2)}, u32[]{:S(2)}) collective-permute-start(s16[16,2176]{1,0:T(8,128)(2,1)S(1)} %get-tuple-element.20), channel_id=1, source_target_pairs={{0,128},{32,160},{64,192},{96,224},{128,256},{160,288},{192,320},{... | collective-permute-start | bytes 208904 | tf_op jit(solution)/shard_map/ppermute | solution.py:153
  71.3 5.9 %collective-permute-start.6 = (s16[16,2176]{1,0:T(8,128)(2,1)S(1)}, s16[16,2176]{1,0:T(8,128)(2,1)S(1)}, u32[]{:S(2)}, u32[]{:S(2)}) collective-permute-start(s16[16,2176]{1,0:T(8,128)(2,1)S(1)} %get-tuple-element.21), channel_id=1, source_target_pairs={{0,384},{32,416},{64,448},{96,480},{128,0},{160,32},{192,64},{224,... | collective-permute-start | bytes 208904 | tf_op jit(solution)/shard_map/ppermute | solution.py:153
  77.2 0.0 collective-permute-done.4.a_ref
  77.3 4.0 %collective-permute-done.5.b_ref = s16[16,2176]{1,0:T(8,128)(2,1)S(1)} collective-permute-done((s16[16,2176]{1,0:T(8,128)(2,1)S(1)}, s16[16,2176]{1,0:T(8,128)(2,1)S(1)}, u32[]{:S(2)}, u32[]{:S(2)}) %collective-permute-start.5) | collective-permute-done | bytes 69664 | tf_op jit(solution)/shard_map/ppermute | solution.py:153
  81.3 0.5 collective-permute-done.6.c_ref
  81.8 0.4 shard_map.70
  82.1 12.1 %all_to_all.15.stats_ref = f32[32,1,384]{2,1,0:T(1,128)S(1)} all-to-all(f32[32,1,384]{2,1,0:T(1,128)S(1)} %get-tuple-element.23), channel_id=1, replica_groups=mesh['rows'=16,'vocab'=32] {'vocab'}, dimensions={0} | all-to-all | bytes 98304 | tf_op jit(solution)/shard_map/all_to_all | solution.py:148
  94.2 0.8 shard_map.71
  (5 shorter events, 0.0 us)
Async XLA Ops:
  0.6 52.7 %copy-start = (s32[24,128]{1,0:T(8,128)S(1)}, s32[24,128]{1,0:T(8,128)}, u32[]{:S(2)}) copy-start(s32[24,128]{1,0:T(8,128)} %param.7) | copy-start | bytes 36868
  0.6 52.6 %copy-start.1 = (s32[1,8]{1,0:T(1,128)S(1)}, s32[1,8]{1,0:T(1,128)}, u32[]{:S(2)}) copy-start(s32[1,8]{1,0:T(1,128)} %param.8) | copy-start | bytes 100
  0.7 18.4 %all-to-all-start = ((bf16[32,16,128]{2,1,0:T(8,128)(2,1)}), bf16[32,16,128]{2,1,0:T(8,128)(2,1)S(1)}, u32[]{:S(2)}, u32[]{:S(2)}) async-start(bf16[32,16,128]{2,1,0:T(8,128)(2,1)} %bitcast.16), calls=%async_computation | async-start | bytes 262144 | tf_op jit(solution)/shard_map/all_to_all | solution.py:148
  19.7 11.7 %all-to-all-start.1 = ((bf16[32,16,128]{2,1,0:T(8,128)(2,1)}), bf16[32,16,128]{2,1,0:T(8,128)(2,1)S(1)}, u32[]{:S(2)}, u32[]{:S(2)}) async-start(bf16[32,16,128]{2,1,0:T(8,128)(2,1)} %broadcast_in_dim.15), calls=%async_computation.1 | async-start | bytes 262144 | tf_op jit(solution)/shard_map/all_to_all | solution.py:148
  34.7 23.1 %collective-permute-start = (s16[32,4224]{1,0:T(8,128)(2,1)S(1)}, s16[32,4224]{1,0:T(8,128)(2,1)S(1)}, u32[]{:S(2)}, u32[]{:S(2)}) collective-permute-start(s16[32,4224]{1,0:T(8,128)(2,1)S(1)} %get-tuple-element.14), channel_id=1, source_target_pairs={{0,32},{32,64},{64,96},{96,128},{128,160},{160,192},{192,224},{224... | collective-permute-start | bytes 811016 | tf_op jit(solution)/shard_map/ppermute | solution.py:153
  36.6 21.2 %collective-permute-start.1 = (s16[32,4224]{1,0:T(8,128)(2,1)S(1)}, s16[32,4224]{1,0:T(8,128)(2,1)S(1)}, u32[]{:S(2)}, u32[]{:S(2)}) collective-permute-start(s16[32,4224]{1,0:T(8,128)(2,1)S(1)} %get-tuple-element.15), channel_id=1, source_target_pairs={{0,480},{32,0},{64,32},{96,64},{128,96},{160,128},{192,160},{224,1... | collective-permute-start | bytes 811016 | tf_op jit(solution)/shard_map/ppermute | solution.py:153
  45.8 11.4 %collective-permute-start.2 = (s16[32,2176]{1,0:T(8,128)(2,1)S(1)}, s16[32,2176]{1,0:T(8,128)(2,1)S(1)}, u32[]{:S(2)}, u32[]{:S(2)}) collective-permute-start(s16[32,2176]{1,0:T(8,128)(2,1)S(1)} %get-tuple-element.16), channel_id=1, source_target_pairs={{0,64},{32,96},{64,128},{96,160},{128,192},{160,224},{192,256},{22... | collective-permute-start | bytes 417800 | tf_op jit(solution)/shard_map/ppermute | solution.py:153
  47.8 10.0 %collective-permute-start.3 = (s16[32,2176]{1,0:T(8,128)(2,1)S(1)}, s16[32,2176]{1,0:T(8,128)(2,1)S(1)}, u32[]{:S(2)}, u32[]{:S(2)}) collective-permute-start(s16[32,2176]{1,0:T(8,128)(2,1)S(1)} %get-tuple-element.17), channel_id=1, source_target_pairs={{0,448},{32,480},{64,0},{96,32},{128,64},{160,96},{192,128},{224,1... | collective-permute-start | bytes 417800 | tf_op jit(solution)/shard_map/ppermute | solution.py:153
  58.2 19.1 %collective-permute-start.4 = (s16[16,2176]{1,0:T(8,128)(2,1)S(1)}, s16[16,2176]{1,0:T(8,128)(2,1)S(1)}, u32[]{:S(2)}, u32[]{:S(2)}) collective-permute-start(s16[16,2176]{1,0:T(8,128)(2,1)S(1)} %get-tuple-element.19), channel_id=1, source_target_pairs={{0,256},{32,288},{64,320},{96,352},{128,384},{160,416},{192,448},{... | collective-permute-start | bytes 208904 | tf_op jit(solution)/shard_map/ppermute | solution.py:153
  68.0 13.3 %collective-permute-start.5 = (s16[16,2176]{1,0:T(8,128)(2,1)S(1)}, s16[16,2176]{1,0:T(8,128)(2,1)S(1)}, u32[]{:S(2)}, u32[]{:S(2)}) collective-permute-start(s16[16,2176]{1,0:T(8,128)(2,1)S(1)} %get-tuple-element.20), channel_id=1, source_target_pairs={{0,128},{32,160},{64,192},{96,224},{128,256},{160,288},{192,320},{... | collective-permute-start | bytes 208904 | tf_op jit(solution)/shard_map/ppermute | solution.py:153
  71.3 10.5 %collective-permute-start.6 = (s16[16,2176]{1,0:T(8,128)(2,1)S(1)}, s16[16,2176]{1,0:T(8,128)(2,1)S(1)}, u32[]{:S(2)}, u32[]{:S(2)}) collective-permute-start(s16[16,2176]{1,0:T(8,128)(2,1)S(1)} %get-tuple-element.21), channel_id=1, source_target_pairs={{0,384},{32,416},{64,448},{96,480},{128,0},{160,32},{192,64},{224,... | collective-permute-start | bytes 208904 | tf_op jit(solution)/shard_map/ppermute | solution.py:153

commit v3 on v2

--- a/solution.py
+++ b/solution.py
@@ -32,7 +32,7 @@
     return jnp.exp2(0.125 * to_f32(codes)[:, :1])
 
 
-def product_kernel(z_ref, x_ref, w_ref, own_ref, up_ref, down_ref, up2_ref, down2_ref, acc_ref, held_ref, sems):
+def product_kernel(z_ref, x_ref, w_ref, own_ref, up_ref, up2_ref, down_ref, acc_ref, held_ref, sems):
     def tile(t):
         part = pl.ds(t * WIDE, WIDE)
         return pltpu.make_async_copy(w_ref.at[:, part], held_ref.at[:, part], sems.at[t])
@@ -45,7 +45,7 @@
     i = lax.broadcasted_iota(jnp.int32, (128, 128), 0)
     source = lax.broadcasted_iota(jnp.int32, (128, 128), 1)
     b = i >> 5
-    piece = (z_ref[0] + jnp.where(b == 3, -1, b) + 4 * ((i >> 3) & 3)) & 15
+    piece = (z_ref[0] + z_ref[1] * (jnp.where(b == 3, -1, b) + 4 * ((i >> 3) & 3))) & 15
     chosen = (source == 8 * piece + (i & 7)).astype(F32).astype(jnp.bfloat16)
     x = jnp.dot(chosen, x, preferred_element_type=F32).astype(jnp.bfloat16)
     for t in range(TILES):
@@ -54,20 +54,14 @@
             x, held_ref[:, t * WIDE : (t + 1) * WIDE], preferred_element_type=F32
         )
     own_ref[...] = acc_ref[:32]
-    for ref, lo in ((up_ref, 32), (down_ref, 96)):
+    for ref, lo in ((up_ref, 32), (up2_ref, 64), (down_ref, 96)):
         q, k = encode(acc_ref[lo : lo + 32])
         ref[:, :N] = to_i16(q)
         ref[:, N:] = to_i16(jnp.broadcast_to(k, (32, TAIL)))
-    q, k = encode(acc_ref[64:96])
-    tail = to_i16(jnp.broadcast_to(k, (32, TAIL)))
-    up2_ref[:, :HALF] = to_i16(q[:, :HALF])
-    up2_ref[:, HALF:] = tail
-    down2_ref[:, :HALF] = to_i16(q[:, HALF:])
-    down2_ref[:, HALF:] = tail
 
 
 def product(z, x, w):
-    outs = ((32, N), (32, N + TAIL), (32, N + TAIL), (32, HALF + TAIL), (32, HALF + TAIL))
+    outs = ((32, N), (32, N + TAIL), (32, N + TAIL), (32, N + TAIL))
     return pl.pallas_call(
         product_kernel,
         in_specs=[
@@ -86,16 +80,10 @@
     )(z, x, w)
 
 
-def first_sum_kernel(own_ref, low_ref, high_ref, low2_ref, high2_ref, keep_ref, up_ref, far_ref, down_ref):
-    near = (
-        own_ref[...]
-        + to_f32(low_ref[:, :N]) * scale_of(low_ref[:, N:])
-        + to_f32(high_ref[:, :N]) * scale_of(high_ref[:, N:])
-    )
-    left = to_f32(low2_ref[:, :HALF]) * scale_of(low2_ref[:, HALF:])
-    right = to_f32(high2_ref[:, :HALF]) * scale_of(high2_ref[:, HALF:])
-    right = jnp.concatenate([right[24:], right[:24]], axis=0)
-    total = near + jnp.concatenate([left, right], axis=1)
+def first_sum_kernel(own_ref, a_ref, b_ref, c_ref, keep_ref, up_ref, far_ref, down_ref):
+    total = own_ref[...]
+    for ref in (a_ref, b_ref, c_ref):
+        total = total + to_f32(ref[:, :N]) * scale_of(ref[:, N:])
     keep_ref[...] = total[:8]
     for ref, lo in ((up_ref, 8), (far_ref, 16), (down_ref, 24)):
         q, k = encode(total[lo : lo + 8])
@@ -149,19 +137,23 @@
 
 
 def shift(array, step):
-    count = lax.axis_size("rows")
-    return lax.ppermute(array, "rows", [(i, (i + step) % count) for i in range(count)])
+    rows, columns = lax.axis_size("rows"), lax.axis_size("vocab")
+    pairs = [
+        (z * columns + v, (z + (step if v % 2 == 0 else -step)) % rows * columns + v)
+        for z in range(rows)
+        for v in range(columns)
+    ]
+    return lax.ppermute(array, ("rows", "vocab"), pairs)
 
 
 def shards(hidden_held, head_weight, state_table, row_states, owner):
-    z = lax.axis_index("rows").astype(jnp.int32)[None]
+    z = jnp.stack([lax.axis_index("rows"), 1 - 2 * (lax.axis_index("vocab") % 2)]).astype(jnp.int32)
     chunks = hidden_held[0, 0].reshape(16, 8, 4, 128).transpose(0, 2, 1, 3).reshape(32, 16, 128)
     mine = lax.dynamic_index_in_dim(spread(chunks, "vocab"), owner[0], 0, keepdims=True)
     x = spread(jnp.broadcast_to(mine, (32, 16, 128)), "vocab")
 
-    own, up, down, up2, down2 = product(z, x, head_weight)
-    low2, low, high, high2 = shift(up2, 2), shift(up, 1), shift(down, -1), shift(down2, -2)
-    own, up, far, down = first_sum(own, low, high, low2, high2)
+    own, up, up2, down = product(z, x, head_weight)
+    own, up, far, down = first_sum(own, shift(up, 1), shift(up2, 2), shift(down, -1))
 
     words = state_table[row_states[0]]
     bits = jnp.right_shift(words[:, :, None], jnp.arange(32, dtype=jnp.int32)) & 1

time: 96.3 us -> 95.9 us (level)
  starting transfers between devices: 52 us -> 47.5 us
  blocking collectives: 12.1 us -> 15.1 us
  waiting for transfers between devices: 22.9 us -> 24.1 us
    ppermute x7 -> x6, starting transfers between devices: 37.5 us -> 33.1 us  [shift(): return lax.ppermute(array, ('rows', 'vocab'), pairs)]
    all_to_all x1, blocking collectives: 12.1 us -> 15.1 us  [spread(): return lax.all_to_all(array, axis, 0, 0)]
    ppermute x7 -> x6, waiting for transfers between devices: 7.93 us -> 9.25 us  [shift(): return lax.ppermute(array, ('rows', 'vocab'), pairs)]
  transfers between devices with their start and end apart: 9 -> 8, of which waited for: 6 -> 5; matrix products, arithmetic and copies ran while one was open for 1% -> 1% of each run, Pallas kernels for 0% -> 0%
where the time goes in v3:
time: 95.9 us; the launch traced here: 95.4 us
  starting transfers between devices  47.5 us (50%)
  waiting for transfers between devices  24.1 us (25%)
  blocking collectives  15.1 us (16%)
  Pallas kernels  5.35 us (6%)
  local copies, waits for them, and re-layouts  1.76 us (2%)
  between operations  1.47 us (2%)
    ppermute x6, starting transfers between devices, shift(): return lax.ppermute(array, ('rows', 'vocab'), pairs)  33.1 us
    all_to_all x1, blocking collectives, spread(): return lax.all_to_all(array, axis, 0, 0)  15.1 us
    all_to_all x2, waiting for transfers between devices, spread(): return lax.all_to_all(array, axis, 0, 0)  14.9 us
    all_to_all x2, starting transfers between devices, spread(): return lax.all_to_all(array, axis, 0, 0)  14.4 us
    ppermute x6, waiting for transfers between devices, shift(): return lax.ppermute(array, ('rows', 'vocab'), pairs)  9.25 us
    pallas_call x1, Pallas kernels, product(): pl.pallas_call(product_kernel, in_specs=[pl.BlockSpec(memory_space=pltpu....  3.81 us
  transfers between devices with their start and end apart: 8, of which 5 were waited for; matrix products, arithmetic and copies ran while one was open for 1% of the time, Pallas kernels for 0%

profile of v3, /device:TPU:1, one launch (start us, length us, event | category | flops | bytes accessed | tf_op | source)
XLA Modules:
  0.0 95.4 jit_solution(7967697187993352868)
XLA Ops:
  0.6 0.0 copy-start
  0.6 0.0 copy-start.1
  0.7 10.5 %all-to-all-start = ((bf16[32,16,128]{2,1,0:T(8,128)(2,1)}), bf16[32,16,128]{2,1,0:T(8,128)(2,1)S(1)}, u32[]{:S(2)}, u32[]{:S(2)}) async-start(bf16[32,16,128]{2,1,0:T(8,128)(2,1)} %bitcast.17), calls=%async_computation | async-start | bytes 262144 | tf_op jit(solution)/shard_map/all_to_all | solution.py:136
  11.8 7.2 %all-to-all-done = bf16[32,16,128]{2,1,0:T(8,128)(2,1)S(1)} async-done(((bf16[32,16,128]{2,1,0:T(8,128)(2,1)}), bf16[32,16,128]{2,1,0:T(8,128)(2,1)S(1)}, u32[]{:S(2)}, u32[]{:S(2)}) %all-to-all-start) | async-done | bytes 131104 | tf_op jit(solution)/shard_map/all_to_all | solution.py:136
  19.0 0.7 broadcast_in_dim.5
  19.7 3.9 %all-to-all-start.1 = ((bf16[32,16,128]{2,1,0:T(8,128)(2,1)}), bf16[32,16,128]{2,1,0:T(8,128)(2,1)S(1)}, u32[]{:S(2)}, u32[]{:S(2)}) async-start(bf16[32,16,128]{2,1,0:T(8,128)(2,1)} %broadcast_in_dim.5), calls=%async_computation.1 | async-start | bytes 262144 | tf_op jit(solution)/shard_map/all_to_all | solution.py:136
  23.6 0.1 pad_add_fusion.z_ref
  23.7 7.7 %all-to-all-done.1.x_ref = bf16[32,16,128]{2,1,0:T(8,128)(2,1)S(1)} async-done(((bf16[32,16,128]{2,1,0:T(8,128)(2,1)}), bf16[32,16,128]{2,1,0:T(8,128)(2,1)S(1)}, u32[]{:S(2)}, u32[]{:S(2)}) %all-to-all-start.1) | async-done | bytes 131104 | tf_op jit(solution)/shard_map/all_to_all | solution.py:136
  31.4 3.8 %shard_map.68 = (f32[32,4096]{1,0:T(8,128)S(1)}, s16[32,4224]{1,0:T(8,128)(2,1)S(1)}, s16[32,4224]{1,0:T(8,128)(2,1)S(1)}, s16[32,4224]{1,0:T(8,128)(2,1)S(1)}) custom-call(s32[2]{0:T(128)S(1)} %pad_add_fusion.z_ref, bf16[32,16,128]{2,1,0:T(8,128)(2,1)S(1)} %all-to-all-done.1.x_ref, bf16[512,4096]{1,0:T(8,128)(2,1)} %w_ref.1), custom_call_target="tpu_custom_call" | custom-call | flops 536870912 | bytes 6291456 | tf_op jit(solution)/shard_map/pallas_call | solution.py:65
  35.2 9.2 %collective-permute-start = (s16[32,4224]{1,0:T(8,128)(2,1)S(1)}, s16[32,4224]{1,0:T(8,128)(2,1)S(1)}, u32[]{:S(2)}, u32[]{:S(2)}) collective-permute-start(s16[32,4224]{1,0:T(8,128)(2,1)S(1)} %get-tuple-element.13), channel_id=1, source_target_pairs={{0,32},{1,481},{2,34},{3,483},{4,36},{5,485},{6,38},{7,487},{8,40}... | collective-permute-start | bytes 811016 | tf_op jit(solution)/shard_map/ppermute | solution.py:146
  44.5 3.1 %collective-permute-start.1 = (s16[32,4224]{1,0:T(8,128)(2,1)S(1)}, s16[32,4224]{1,0:T(8,128)(2,1)S(1)}, u32[]{:S(2)}, u32[]{:S(2)}) collective-permute-start(s16[32,4224]{1,0:T(8,128)(2,1)S(1)} %get-tuple-element.14), channel_id=1, source_target_pairs={{0,64},{1,449},{2,66},{3,451},{4,68},{5,453},{6,70},{7,455},{8,72}... | collective-permute-start | bytes 811016 | tf_op jit(solution)/shard_map/ppermute | solution.py:146
  47.5 2.6 %collective-permute-start.2 = (s16[32,4224]{1,0:T(8,128)(2,1)S(1)}, s16[32,4224]{1,0:T(8,128)(2,1)S(1)}, u32[]{:S(2)}, u32[]{:S(2)}) collective-permute-start(s16[32,4224]{1,0:T(8,128)(2,1)S(1)} %get-tuple-element.15), channel_id=1, source_target_pairs={{0,480},{1,33},{2,482},{3,35},{4,484},{5,37},{6,486},{7,39},{8,488... | collective-permute-start | bytes 811016 | tf_op jit(solution)/shard_map/ppermute | solution.py:146
  50.2 0.0 copy-done.1
  50.2 0.0 copy-done
  50.2 0.6 gather_fusion
  50.8 0.2 shift_right_arithmetic.20
  51.0 0.2 shift_right_arithmetic.21
  51.3 0.1 shift_right_arithmetic.23
  51.3 0.0 collective-permute-done.a_ref
  51.3 4.1 %collective-permute-done.1.b_ref = s16[32,4224]{1,0:T(8,128)(2,1)S(1)} collective-permute-done((s16[32,4224]{1,0:T(8,128)(2,1)S(1)}, s16[32,4224]{1,0:T(8,128)(2,1)S(1)}, u32[]{:S(2)}, u32[]{:S(2)}) %collective-permute-start.1) | collective-permute-done | bytes 270368 | tf_op jit(solution)/shard_map/ppermute | solution.py:146
  55.4 2.1 %collective-permute-done.2.c_ref = s16[32,4224]{1,0:T(8,128)(2,1)S(1)} collective-permute-done((s16[32,4224]{1,0:T(8,128)(2,1)S(1)}, s16[32,4224]{1,0:T(8,128)(2,1)S(1)}, u32[]{:S(2)}, u32[]{:S(2)}) %collective-permute-start.2) | collective-permute-done | bytes 270368 | tf_op jit(solution)/shard_map/ppermute | solution.py:146
  57.6 0.4 shard_map.69
  57.9 9.0 %collective-permute-start.3 = (s16[16,2176]{1,0:T(8,128)(2,1)S(1)}, s16[16,2176]{1,0:T(8,128)(2,1)S(1)}, u32[]{:S(2)}, u32[]{:S(2)}) collective-permute-start(s16[16,2176]{1,0:T(8,128)(2,1)S(1)} %get-tuple-element.17), channel_id=1, source_target_pairs={{0,256},{1,257},{2,258},{3,259},{4,260},{5,261},{6,262},{7,263},{8... | collective-permute-start | bytes 208904 | tf_op jit(solution)/shard_map/ppermute | solution.py:146
  66.9 1.9 %collective-permute-start.4 = (s16[16,2176]{1,0:T(8,128)(2,1)S(1)}, s16[16,2176]{1,0:T(8,128)(2,1)S(1)}, u32[]{:S(2)}, u32[]{:S(2)}) collective-permute-start(s16[16,2176]{1,0:T(8,128)(2,1)S(1)} %get-tuple-element.18), channel_id=1, source_target_pairs={{0,128},{1,385},{2,130},{3,387},{4,132},{5,389},{6,134},{7,391},{8... | collective-permute-start | bytes 208904 | tf_op jit(solution)/shard_map/ppermute | solution.py:146
  68.8 7.3 %collective-permute-start.5 = (s16[16,2176]{1,0:T(8,128)(2,1)S(1)}, s16[16,2176]{1,0:T(8,128)(2,1)S(1)}, u32[]{:S(2)}, u32[]{:S(2)}) collective-permute-start(s16[16,2176]{1,0:T(8,128)(2,1)S(1)} %get-tuple-element.19), channel_id=1, source_target_pairs={{0,384},{1,129},{2,386},{3,131},{4,388},{5,133},{6,390},{7,135},{8... | collective-permute-start | bytes 208904 | tf_op jit(solution)/shard_map/ppermute | solution.py:146
  76.1 0.0 collective-permute-done.3.a_ref
  76.1 3.0 %collective-permute-done.4.b_ref = s16[16,2176]{1,0:T(8,128)(2,1)S(1)} collective-permute-done((s16[16,2176]{1,0:T(8,128)(2,1)S(1)}, s16[16,2176]{1,0:T(8,128)(2,1)S(1)}, u32[]{:S(2)}, u32[]{:S(2)}) %collective-permute-start.4) | collective-permute-done | bytes 69664 | tf_op jit(solution)/shard_map/ppermute | solution.py:146
  79.2 0.0 collective-permute-done.5.c_ref
  79.2 0.4 shard_map.70
  79.5 15.1 %all_to_all.15.stats_ref = f32[32,1,384]{2,1,0:T(1,128)S(1)} all-to-all(f32[32,1,384]{2,1,0:T(1,128)S(1)} %get-tuple-element.21), channel_id=1, replica_groups=mesh['rows'=16,'vocab'=32] {'vocab'}, dimensions={0} | all-to-all | bytes 98304 | tf_op jit(solution)/shard_map/all_to_all | solution.py:136
  94.6 0.8 shard_map.71
  (5 shorter events, 0.0 us)
Async XLA Ops:
  0.6 49.6 %copy-start = (s32[24,128]{1,0:T(8,128)S(1)}, s32[24,128]{1,0:T(8,128)}, u32[]{:S(2)}) copy-start(s32[24,128]{1,0:T(8,128)} %param.7) | copy-start | bytes 36868
  0.6 49.6 %copy-start.1 = (s32[1,8]{1,0:T(1,128)S(1)}, s32[1,8]{1,0:T(1,128)}, u32[]{:S(2)}) copy-start(s32[1,8]{1,0:T(1,128)} %param.8) | copy-start | bytes 100
  0.7 18.4 %all-to-all-start = ((bf16[32,16,128]{2,1,0:T(8,128)(2,1)}), bf16[32,16,128]{2,1,0:T(8,128)(2,1)S(1)}, u32[]{:S(2)}, u32[]{:S(2)}) async-start(bf16[32,16,128]{2,1,0:T(8,128)(2,1)} %bitcast.17), calls=%async_computation | async-start | bytes 262144 | tf_op jit(solution)/shard_map/all_to_all | solution.py:136
  19.7 11.7 %all-to-all-start.1 = ((bf16[32,16,128]{2,1,0:T(8,128)(2,1)}), bf16[32,16,128]{2,1,0:T(8,128)(2,1)S(1)}, u32[]{:S(2)}, u32[]{:S(2)}) async-start(bf16[32,16,128]{2,1,0:T(8,128)(2,1)} %broadcast_in_dim.5), calls=%async_computation.1 | async-start | bytes 262144 | tf_op jit(solution)/shard_map/all_to_all | solution.py:136
  35.2 16.1 %collective-permute-start = (s16[32,4224]{1,0:T(8,128)(2,1)S(1)}, s16[32,4224]{1,0:T(8,128)(2,1)S(1)}, u32[]{:S(2)}, u32[]{:S(2)}) collective-permute-start(s16[32,4224]{1,0:T(8,128)(2,1)S(1)} %get-tuple-element.13), channel_id=1, source_target_pairs={{0,32},{1,481},{2,34},{3,483},{4,36},{5,485},{6,38},{7,487},{8,40}... | collective-permute-start | bytes 811016 | tf_op jit(solution)/shard_map/ppermute | solution.py:146
  44.5 11.0 %collective-permute-start.1 = (s16[32,4224]{1,0:T(8,128)(2,1)S(1)}, s16[32,4224]{1,0:T(8,128)(2,1)S(1)}, u32[]{:S(2)}, u32[]{:S(2)}) collective-permute-start(s16[32,4224]{1,0:T(8,128)(2,1)S(1)} %get-tuple-element.14), channel_id=1, source_target_pairs={{0,64},{1,449},{2,66},{3,451},{4,68},{5,453},{6,70},{7,455},{8,72}... | collective-permute-start | bytes 811016 | tf_op jit(solution)/shard_map/ppermute | solution.py:146
  47.5 10.0 %collective-permute-start.2 = (s16[32,4224]{1,0:T(8,128)(2,1)S(1)}, s16[32,4224]{1,0:T(8,128)(2,1)S(1)}, u32[]{:S(2)}, u32[]{:S(2)}) collective-permute-start(s16[32,4224]{1,0:T(8,128)(2,1)S(1)} %get-tuple-element.15), channel_id=1, source_target_pairs={{0,480},{1,33},{2,482},{3,35},{4,484},{5,37},{6,486},{7,39},{8,488... | collective-permute-start | bytes 811016 | tf_op jit(solution)/shard_map/ppermute | solution.py:146
  57.9 18.2 %collective-permute-start.3 = (s16[16,2176]{1,0:T(8,128)(2,1)S(1)}, s16[16,2176]{1,0:T(8,128)(2,1)S(1)}, u32[]{:S(2)}, u32[]{:S(2)}) collective-permute-start(s16[16,2176]{1,0:T(8,128)(2,1)S(1)} %get-tuple-element.17), channel_id=1, source_target_pairs={{0,256},{1,257},{2,258},{3,259},{4,260},{5,261},{6,262},{7,263},{8... | collective-permute-start | bytes 208904 | tf_op jit(solution)/shard_map/ppermute | solution.py:146
  66.9 12.3 %collective-permute-start.4 = (s16[16,2176]{1,0:T(8,128)(2,1)S(1)}, s16[16,2176]{1,0:T(8,128)(2,1)S(1)}, u32[]{:S(2)}, u32[]{:S(2)}) collective-permute-start(s16[16,2176]{1,0:T(8,128)(2,1)S(1)} %get-tuple-element.18), channel_id=1, source_target_pairs={{0,128},{1,385},{2,130},{3,387},{4,132},{5,389},{6,134},{7,391},{8... | collective-permute-start | bytes 208904 | tf_op jit(solution)/shard_map/ppermute | solution.py:146
  68.8 10.3 %collective-permute-start.5 = (s16[16,2176]{1,0:T(8,128)(2,1)S(1)}, s16[16,2176]{1,0:T(8,128)(2,1)S(1)}, u32[]{:S(2)}, u32[]{:S(2)}) collective-permute-start(s16[16,2176]{1,0:T(8,128)(2,1)S(1)} %get-tuple-element.19), channel_id=1, source_target_pairs={{0,384},{1,129},{2,386},{3,131},{4,388},{5,133},{6,390},{7,135},{8... | collective-permute-start | bytes 208904 | tf_op jit(solution)/shard_map/ppermute | solution.py:146

commit v4 on v3

--- a/solution.py
+++ b/solution.py
@@ -45,7 +45,7 @@
     i = lax.broadcasted_iota(jnp.int32, (128, 128), 0)
     source = lax.broadcasted_iota(jnp.int32, (128, 128), 1)
     b = i >> 5
-    piece = (z_ref[0] + z_ref[1] * (jnp.where(b == 3, -1, b) + 4 * ((i >> 3) & 3))) & 15
+    piece = ((z_ref[0] & 15) + (1 - 2 * (z_ref[0] >> 4)) * (jnp.where(b == 3, -1, b) + 4 * ((i >> 3) & 3))) & 15
     chosen = (source == 8 * piece + (i & 7)).astype(F32).astype(jnp.bfloat16)
     x = jnp.dot(chosen, x, preferred_element_type=F32).astype(jnp.bfloat16)
     for t in range(TILES):
@@ -80,32 +80,46 @@
     )(z, x, w)
 
 
+def pack(ref, values):
+    q, k = encode(values)
+    ref[:, :HALF] = to_i16(jnp.concatenate([q[:, :HALF], q[:, HALF:]], axis=0))
+    ref[:, HALF:] = to_i16(jnp.broadcast_to(jnp.concatenate([k, k], axis=0), (16, TAIL)))
+
+
+def unpack(ref):
+    part = to_f32(ref[:, :HALF]) * scale_of(ref[:, HALF:])
+    return jnp.concatenate([part[:8], part[8:]], axis=1)
+
+
 def first_sum_kernel(own_ref, a_ref, b_ref, c_ref, keep_ref, up_ref, far_ref, down_ref):
     total = own_ref[...]
     for ref in (a_ref, b_ref, c_ref):
         total = total + to_f32(ref[:, :N]) * scale_of(ref[:, N:])
     keep_ref[...] = total[:8]
-    for ref, lo in ((up_ref, 8), (far_ref, 16), (down_ref, 24)):
-        q, k = encode(total[lo : lo + 8])
-        ref[:, :HALF] = to_i16(jnp.concatenate([q[:, :HALF], q[:, HALF:]], axis=0))
-        ref[:, HALF:] = to_i16(jnp.broadcast_to(jnp.concatenate([k, k], axis=0), (16, TAIL)))
+    up_ref[...] = total[8:16]
+    pack(far_ref, total[16:24])
+    pack(down_ref, total[24:])
 
 
-def first_sum(*arrays):
-    coded = jax.ShapeDtypeStruct((16, HALF + TAIL), I16)
+def relay_kernel(up_ref, far_ref, out_ref):
+    pack(out_ref, up_ref[...] + unpack(far_ref))
+
+
+ROWS = jax.ShapeDtypeStruct((8, N), F32)
+CODED = jax.ShapeDtypeStruct((16, HALF + TAIL), I16)
+
+
+def call(kernel, outs, *arrays):
     return pl.pallas_call(
-        first_sum_kernel,
-        out_shape=[jax.ShapeDtypeStruct((8, N), F32), coded, coded, coded],
+        kernel,
+        out_shape=outs,
         compiler_params=pltpu.CompilerParams(vmem_limit_bytes=24 * 2**20),
-        cost_estimate=pl.CostEstimate(flops=2**20, bytes_accessed=2 * 2**20, transcendentals=0),
+        cost_estimate=pl.CostEstimate(flops=2**20, bytes_accessed=2**20, transcendentals=0),
     )(*arrays)
 
 
-def stats_kernel(own_ref, a_ref, b_ref, c_ref, allowed_ref, logits_ref, stats_ref):
-    logits = own_ref[...]
-    for ref in (a_ref, b_ref, c_ref):
-        part = to_f32(ref[:, :HALF]) * scale_of(ref[:, HALF:])
-        logits = logits + jnp.concatenate([part[:8], part[8:]], axis=1)
+def stats_kernel(own_ref, a_ref, b_ref, allowed_ref, logits_ref, stats_ref):
+    logits = own_ref[...] + unpack(a_ref) + unpack(b_ref)
     logits_ref[...] = logits
     allowed = allowed_ref[...] > 0.5
     top = jnp.max(jnp.where(allowed, logits, -1e30), axis=1, keepdims=True)
@@ -147,32 +161,26 @@
 
 
 def shards(hidden_held, head_weight, state_table, row_states, owner):
-    z = jnp.stack([lax.axis_index("rows"), 1 - 2 * (lax.axis_index("vocab") % 2)]).astype(jnp.int32)
+    z = (lax.axis_index("rows") + 16 * (lax.axis_index("vocab") & 1)).astype(jnp.int32)[None]
     chunks = hidden_held[0, 0].reshape(16, 8, 4, 128).transpose(0, 2, 1, 3).reshape(32, 16, 128)
     mine = lax.dynamic_index_in_dim(spread(chunks, "vocab"), owner[0], 0, keepdims=True)
     x = spread(jnp.broadcast_to(mine, (32, 16, 128)), "vocab")
 
     own, up, up2, down = product(z, x, head_weight)
-    own, up, far, down = first_sum(own, shift(up, 1), shift(up2, 2), shift(down, -1))
+    parts = (shift(up, 1), shift(up2, 2), shift(down, -1))
+    own, up, far, down = call(first_sum_kernel, [ROWS, ROWS, CODED, CODED], own, *parts)
+    far, down = shift(far, 4), shift(down, -4)
+    up = shift(call(relay_kernel, CODED, up, far), 4)
 
     words = state_table[row_states[0]]
     bits = jnp.right_shift(words[:, :, None], jnp.arange(32, dtype=jnp.int32)) & 1
     allowed = bits.astype(F32).reshape(8, N)
 
-    parts = (shift(far, 8), shift(up, 4), shift(down, -4))
-    logits, stats = pl.pallas_call(
-        stats_kernel,
-        out_shape=[jax.ShapeDtypeStruct((8, N), F32), jax.ShapeDtypeStruct((32, 1, 384), F32)],
-        compiler_params=pltpu.CompilerParams(vmem_limit_bytes=24 * 2**20),
-    )(own, *parts, allowed)
+    outs = [ROWS, jax.ShapeDtypeStruct((32, 1, 384), F32)]
+    logits, stats = call(stats_kernel, outs, own, down, up, allowed)
     stats = spread(stats, "vocab")
-    return tuple(
-        pl.pallas_call(
-            finish_kernel,
-            out_shape=[jax.ShapeDtypeStruct((1, 8, N), F32), jax.ShapeDtypeStruct((1, 8), F32)],
-            compiler_params=pltpu.CompilerParams(vmem_limit_bytes=24 * 2**20),
-        )(logits, allowed, stats)
-    )
+    outs = [jax.ShapeDtypeStruct((1, 8, N), F32), jax.ShapeDtypeStruct((1, 8), F32)]
+    return tuple(call(finish_kernel, outs, logits, allowed, stats))
 
 
 def solution(mesh):

time: 95.9 us -> 93.4 us (0.974)
  starting transfers between devices: 47.5 us -> 45.2 us
  waiting for transfers between devices: 24.1 us -> 25.9 us
  blocking collectives: 15.1 us -> 13.5 us
    ppermute x6, starting transfers between devices: 33.1 us -> 30.8 us  [shift(): return lax.ppermute(array, ('rows', 'vocab'), pairs)]
    ppermute x6, waiting for transfers between devices: 9.25 us -> 10.9 us  [shift(): return lax.ppermute(array, ('rows', 'vocab'), pairs)]
    all_to_all x1, blocking collectives: 15.1 us -> 13.5 us  [spread(): return lax.all_to_all(array, axis, 0, 0)]
  transfers between devices with their start and end apart: 8 -> 8, of which waited for: 5 -> 6; matrix products, arithmetic and copies ran while one was open for 1% -> 1% of each run, Pallas kernels for 0% -> 0%
where the time goes in v4:
time: 93.4 us; the launch traced here: 92.9 us
  starting transfers between devices  45.2 us (48%)
  waiting for transfers between devices  25.9 us (28%)
  blocking collectives  13.5 us (14%)
  Pallas kernels  5.02 us (5%)
  local copies, waits for them, and re-layouts  1.76 us (2%)
  between operations  1.47 us (2%)
    ppermute x6, starting transfers between devices, shift(): return lax.ppermute(array, ('rows', 'vocab'), pairs)  30.8 us
    all_to_all x2, waiting for transfers between devices, spread(): return lax.all_to_all(array, axis, 0, 0)  15 us
    all_to_all x2, starting transfers between devices, spread(): return lax.all_to_all(array, axis, 0, 0)  14.4 us
    all_to_all x1, blocking collectives, spread(): return lax.all_to_all(array, axis, 0, 0)  13.5 us
    ppermute x6, waiting for transfers between devices, shift(): return lax.ppermute(array, ('rows', 'vocab'), pairs)  10.9 us
    pallas_call x1, Pallas kernels, product(): pl.pallas_call(product_kernel, in_specs=[pl.BlockSpec(memory_space=pltpu....  3.27 us
  transfers between devices with their start and end apart: 8, of which 6 were waited for; matrix products, arithmetic and copies ran while one was open for 1% of the time, Pallas kernels for 0%

profile of v4, /device:TPU:1, one launch (start us, length us, event | category | flops | bytes accessed | tf_op | source)
XLA Modules:
  0.0 92.9 jit_solution(4575539729786249542)
XLA Ops:
  0.6 0.0 copy-start
  0.6 0.0 copy-start.1
  0.7 10.5 %all-to-all-start = ((bf16[32,16,128]{2,1,0:T(8,128)(2,1)}), bf16[32,16,128]{2,1,0:T(8,128)(2,1)S(1)}, u32[]{:S(2)}, u32[]{:S(2)}) async-start(bf16[32,16,128]{2,1,0:T(8,128)(2,1)} %bitcast.16), calls=%async_computation | async-start | bytes 262144 | tf_op jit(solution)/shard_map/all_to_all | solution.py:150
  11.8 7.2 %all-to-all-done = bf16[32,16,128]{2,1,0:T(8,128)(2,1)S(1)} async-done(((bf16[32,16,128]{2,1,0:T(8,128)(2,1)}), bf16[32,16,128]{2,1,0:T(8,128)(2,1)S(1)}, u32[]{:S(2)}, u32[]{:S(2)}) %all-to-all-start) | async-done | bytes 131104 | tf_op jit(solution)/shard_map/all_to_all | solution.py:150
  19.0 0.7 broadcast_in_dim.15
  19.7 3.9 %all-to-all-start.1 = ((bf16[32,16,128]{2,1,0:T(8,128)(2,1)}), bf16[32,16,128]{2,1,0:T(8,128)(2,1)S(1)}, u32[]{:S(2)}, u32[]{:S(2)}) async-start(bf16[32,16,128]{2,1,0:T(8,128)(2,1)} %broadcast_in_dim.15), calls=%async_computation.1 | async-start | bytes 262144 | tf_op jit(solution)/shard_map/all_to_all | solution.py:150
  23.6 7.8 %all-to-all-done.1.x_ref = bf16[32,16,128]{2,1,0:T(8,128)(2,1)S(1)} async-done(((bf16[32,16,128]{2,1,0:T(8,128)(2,1)}), bf16[32,16,128]{2,1,0:T(8,128)(2,1)S(1)}, u32[]{:S(2)}, u32[]{:S(2)}) %all-to-all-start.1) | async-done | bytes 131104 | tf_op jit(solution)/shard_map/all_to_all | solution.py:150
  31.4 3.3 %shard_map.68 = (f32[32,4096]{1,0:T(8,128)S(1)}, s16[32,4224]{1,0:T(8,128)(2,1)S(1)}, s16[32,4224]{1,0:T(8,128)(2,1)S(1)}, s16[32,4224]{1,0:T(8,128)(2,1)S(1)}) custom-call(s32[1]{0:T(128)} %bitcast.z_ref, bf16[32,16,128]{2,1,0:T(8,128)(2,1)S(1)} %all-to-all-done.1.x_ref, bf16[512,4096]{1,0:T(8,128)(2,1)} %w_ref.1), custom_call_target="tpu_custom_call" | custom-call | flops 536870912 | bytes 6291456 | tf_op jit(solution)/shard_map/pallas_call | solution.py:65
  34.7 9.2 %collective-permute-start = (s16[32,4224]{1,0:T(8,128)(2,1)S(1)}, s16[32,4224]{1,0:T(8,128)(2,1)S(1)}, u32[]{:S(2)}, u32[]{:S(2)}) collective-permute-start(s16[32,4224]{1,0:T(8,128)(2,1)S(1)} %get-tuple-element.13), channel_id=1, source_target_pairs={{0,32},{1,481},{2,34},{3,483},{4,36},{5,485},{6,38},{7,487},{8,40}... | collective-permute-start | bytes 811016 | tf_op jit(solution)/shard_map/ppermute | solution.py:160
  43.9 3.1 %collective-permute-start.1 = (s16[32,4224]{1,0:T(8,128)(2,1)S(1)}, s16[32,4224]{1,0:T(8,128)(2,1)S(1)}, u32[]{:S(2)}, u32[]{:S(2)}) collective-permute-start(s16[32,4224]{1,0:T(8,128)(2,1)S(1)} %get-tuple-element.14), channel_id=1, source_target_pairs={{0,64},{1,449},{2,66},{3,451},{4,68},{5,453},{6,70},{7,455},{8,72}... | collective-permute-start | bytes 811016 | tf_op jit(solution)/shard_map/ppermute | solution.py:160
  47.0 2.6 %collective-permute-start.2 = (s16[32,4224]{1,0:T(8,128)(2,1)S(1)}, s16[32,4224]{1,0:T(8,128)(2,1)S(1)}, u32[]{:S(2)}, u32[]{:S(2)}) collective-permute-start(s16[32,4224]{1,0:T(8,128)(2,1)S(1)} %get-tuple-element.15), channel_id=1, source_target_pairs={{0,480},{1,33},{2,482},{3,35},{4,484},{5,37},{6,486},{7,39},{8,488... | collective-permute-start | bytes 811016 | tf_op jit(solution)/shard_map/ppermute | solution.py:160
  49.7 0.0 copy-done.1
  49.7 0.0 collective-permute-done.a_ref
  49.7 5.2 %collective-permute-done.1.b_ref = s16[32,4224]{1,0:T(8,128)(2,1)S(1)} collective-permute-done((s16[32,4224]{1,0:T(8,128)(2,1)S(1)}, s16[32,4224]{1,0:T(8,128)(2,1)S(1)}, u32[]{:S(2)}, u32[]{:S(2)}) %collective-permute-start.1) | collective-permute-done | bytes 270368 | tf_op jit(solution)/shard_map/ppermute | solution.py:160
  54.9 2.1 %collective-permute-done.2.c_ref = s16[32,4224]{1,0:T(8,128)(2,1)S(1)} collective-permute-done((s16[32,4224]{1,0:T(8,128)(2,1)S(1)}, s16[32,4224]{1,0:T(8,128)(2,1)S(1)}, u32[]{:S(2)}, u32[]{:S(2)}) %collective-permute-start.2) | collective-permute-done | bytes 270368 | tf_op jit(solution)/shard_map/ppermute | solution.py:160
  57.0 0.4 shard_map.69
  57.4 6.7 %collective-permute-start.4 = (s16[16,2176]{1,0:T(8,128)(2,1)S(1)}, s16[16,2176]{1,0:T(8,128)(2,1)S(1)}, u32[]{:S(2)}, u32[]{:S(2)}) collective-permute-start(s16[16,2176]{1,0:T(8,128)(2,1)S(1)} %get-tuple-element.19), channel_id=1, source_target_pairs={{0,128},{1,385},{2,130},{3,387},{4,132},{5,389},{6,134},{7,391},{8... | collective-permute-start | bytes 208904 | tf_op jit(solution)/shard_map/ppermute | solution.py:160
  64.1 0.0 copy-done
  64.1 0.6 gather_fusion
  64.6 0.2 shift_right_arithmetic.20
  64.8 0.2 shift_right_arithmetic.21
  65.1 0.1 shift_right_arithmetic.23
  65.2 2.5 %collective-permute-start.3 = (s16[16,2176]{1,0:T(8,128)(2,1)S(1)}, s16[16,2176]{1,0:T(8,128)(2,1)S(1)}, u32[]{:S(2)}, u32[]{:S(2)}) collective-permute-start(s16[16,2176]{1,0:T(8,128)(2,1)S(1)} %get-tuple-element.17), channel_id=1, source_target_pairs={{0,384},{1,129},{2,386},{3,131},{4,388},{5,133},{6,390},{7,135},{8... | collective-permute-start | bytes 208904 | tf_op jit(solution)/shard_map/ppermute | solution.py:160
  67.7 0.0 collective-permute-done.4.far_ref
  67.7 0.2 shard_map.70
  68.0 6.7 %collective-permute-start.5 = (s16[16,2176]{1,0:T(8,128)(2,1)S(1)}, s16[16,2176]{1,0:T(8,128)(2,1)S(1)}, u32[]{:S(2)}, u32[]{:S(2)}) collective-permute-start(s16[16,2176]{1,0:T(8,128)(2,1)S(1)} %shard_map.70), channel_id=1, source_target_pairs={{0,128},{1,385},{2,130},{3,387},{4,132},{5,389},{6,134},{7,391},{8... | collective-permute-start | bytes 208904 | tf_op jit(solution)/shard_map/ppermute | solution.py:160
  74.7 1.9 %collective-permute-done.3.a_ref = s16[16,2176]{1,0:T(8,128)(2,1)S(1)} collective-permute-done((s16[16,2176]{1,0:T(8,128)(2,1)S(1)}, s16[16,2176]{1,0:T(8,128)(2,1)S(1)}, u32[]{:S(2)}, u32[]{:S(2)}) %collective-permute-start.3) | collective-permute-done | bytes 69664 | tf_op jit(solution)/shard_map/ppermute | solution.py:160
  76.6 1.7 %collective-permute-done.5.b_ref = s16[16,2176]{1,0:T(8,128)(2,1)S(1)} collective-permute-done((s16[16,2176]{1,0:T(8,128)(2,1)S(1)}, s16[16,2176]{1,0:T(8,128)(2,1)S(1)}, u32[]{:S(2)}, u32[]{:S(2)}) %collective-permute-start.5) | collective-permute-done | bytes 69664 | tf_op jit(solution)/shard_map/ppermute | solution.py:160
  78.3 0.3 shard_map.71
  78.6 13.5 %all_to_all.15.stats_ref = f32[32,1,384]{2,1,0:T(1,128)S(1)} all-to-all(f32[32,1,384]{2,1,0:T(1,128)S(1)} %get-tuple-element.21), channel_id=1, replica_groups=mesh['rows'=16,'vocab'=32] {'vocab'}, dimensions={0} | all-to-all | bytes 98304 | tf_op jit(solution)/shard_map/all_to_all | solution.py:150
  92.1 0.8 shard_map.72
  (5 shorter events, 0.0 us)
Async XLA Ops:
  0.6 63.5 %copy-start = (s32[24,128]{1,0:T(8,128)S(1)}, s32[24,128]{1,0:T(8,128)}, u32[]{:S(2)}) copy-start(s32[24,128]{1,0:T(8,128)} %param.7) | copy-start | bytes 36868
  0.6 49.0 %copy-start.1 = (s32[1,8]{1,0:T(1,128)S(1)}, s32[1,8]{1,0:T(1,128)}, u32[]{:S(2)}) copy-start(s32[1,8]{1,0:T(1,128)} %param.8) | copy-start | bytes 100
  0.7 18.4 %all-to-all-start = ((bf16[32,16,128]{2,1,0:T(8,128)(2,1)}), bf16[32,16,128]{2,1,0:T(8,128)(2,1)S(1)}, u32[]{:S(2)}, u32[]{:S(2)}) async-start(bf16[32,16,128]{2,1,0:T(8,128)(2,1)} %bitcast.16), calls=%async_computation | async-start | bytes 262144 | tf_op jit(solution)/shard_map/all_to_all | solution.py:150
  19.7 11.7 %all-to-all-start.1 = ((bf16[32,16,128]{2,1,0:T(8,128)(2,1)}), bf16[32,16,128]{2,1,0:T(8,128)(2,1)S(1)}, u32[]{:S(2)}, u32[]{:S(2)}) async-start(bf16[32,16,128]{2,1,0:T(8,128)(2,1)} %broadcast_in_dim.15), calls=%async_computation.1 | async-start | bytes 262144 | tf_op jit(solution)/shard_map/all_to_all | solution.py:150
  34.7 15.0 %collective-permute-start = (s16[32,4224]{1,0:T(8,128)(2,1)S(1)}, s16[32,4224]{1,0:T(8,128)(2,1)S(1)}, u32[]{:S(2)}, u32[]{:S(2)}) collective-permute-start(s16[32,4224]{1,0:T(8,128)(2,1)S(1)} %get-tuple-element.13), channel_id=1, source_target_pairs={{0,32},{1,481},{2,34},{3,483},{4,36},{5,485},{6,38},{7,487},{8,40}... | collective-permute-start | bytes 811016 | tf_op jit(solution)/shard_map/ppermute | solution.py:160
  43.9 11.0 %collective-permute-start.1 = (s16[32,4224]{1,0:T(8,128)(2,1)S(1)}, s16[32,4224]{1,0:T(8,128)(2,1)S(1)}, u32[]{:S(2)}, u32[]{:S(2)}) collective-permute-start(s16[32,4224]{1,0:T(8,128)(2,1)S(1)} %get-tuple-element.14), channel_id=1, source_target_pairs={{0,64},{1,449},{2,66},{3,451},{4,68},{5,453},{6,70},{7,455},{8,72}... | collective-permute-start | bytes 811016 | tf_op jit(solution)/shard_map/ppermute | solution.py:160
  47.0 10.0 %collective-permute-start.2 = (s16[32,4224]{1,0:T(8,128)(2,1)S(1)}, s16[32,4224]{1,0:T(8,128)(2,1)S(1)}, u32[]{:S(2)}, u32[]{:S(2)}) collective-permute-start(s16[32,4224]{1,0:T(8,128)(2,1)S(1)} %get-tuple-element.15), channel_id=1, source_target_pairs={{0,480},{1,33},{2,482},{3,35},{4,484},{5,37},{6,486},{7,39},{8,488... | collective-permute-start | bytes 811016 | tf_op jit(solution)/shard_map/ppermute | solution.py:160
  57.4 10.3 %collective-permute-start.4 = (s16[16,2176]{1,0:T(8,128)(2,1)S(1)}, s16[16,2176]{1,0:T(8,128)(2,1)S(1)}, u32[]{:S(2)}, u32[]{:S(2)}) collective-permute-start(s16[16,2176]{1,0:T(8,128)(2,1)S(1)} %get-tuple-element.19), channel_id=1, source_target_pairs={{0,128},{1,385},{2,130},{3,387},{4,132},{5,389},{6,134},{7,391},{8... | collective-permute-start | bytes 208904 | tf_op jit(solution)/shard_map/ppermute | solution.py:160
  65.2 11.4 %collective-permute-start.3 = (s16[16,2176]{1,0:T(8,128)(2,1)S(1)}, s16[16,2176]{1,0:T(8,128)(2,1)S(1)}, u32[]{:S(2)}, u32[]{:S(2)}) collective-permute-start(s16[16,2176]{1,0:T(8,128)(2,1)S(1)} %get-tuple-element.17), channel_id=1, source_target_pairs={{0,384},{1,129},{2,386},{3,131},{4,388},{5,133},{6,390},{7,135},{8... | collective-permute-start | bytes 208904 | tf_op jit(solution)/shard_map/ppermute | solution.py:160
  68.0 10.3 %collective-permute-start.5 = (s16[16,2176]{1,0:T(8,128)(2,1)S(1)}, s16[16,2176]{1,0:T(8,128)(2,1)S(1)}, u32[]{:S(2)}, u32[]{:S(2)}) collective-permute-start(s16[16,2176]{1,0:T(8,128)(2,1)S(1)} %shard_map.70), channel_id=1, source_target_pairs={{0,128},{1,385},{2,130},{3,387},{4,132},{5,389},{6,134},{7,391},{8... | collective-permute-start | bytes 208904 | tf_op jit(solution)/shard_map/ppermute | solution.py:160

commit v5 on v4

--- a/solution.py
+++ b/solution.py
@@ -32,7 +32,7 @@
     return jnp.exp2(0.125 * to_f32(codes)[:, :1])
 
 
-def product_kernel(z_ref, x_ref, w_ref, own_ref, up_ref, up2_ref, down_ref, acc_ref, held_ref, sems):
+def product_kernel(z_ref, x_ref, w_ref, own_ref, down_ref, up2_ref, up_ref, acc_ref, held_ref, sems):
     def tile(t):
         part = pl.ds(t * WIDE, WIDE)
         return pltpu.make_async_copy(w_ref.at[:, part], held_ref.at[:, part], sems.at[t])
@@ -165,16 +165,17 @@
     chunks = hidden_held[0, 0].reshape(16, 8, 4, 128).transpose(0, 2, 1, 3).reshape(32, 16, 128)
     mine = lax.dynamic_index_in_dim(spread(chunks, "vocab"), owner[0], 0, keepdims=True)
     x = spread(jnp.broadcast_to(mine, (32, 16, 128)), "vocab")
-
-    own, up, up2, down = product(z, x, head_weight)
-    parts = (shift(up, 1), shift(up2, 2), shift(down, -1))
+    words = state_table[row_states[0]]
+    bits = jnp.right_shift(words[:, :, None], jnp.arange(32, dtype=jnp.int32)) & 1
+    allowed = bits.astype(F32).reshape(8, N)
+
+    x, allowed = lax.optimization_barrier((x, allowed))
+
+    own, down, up2, up = product(z, x, head_weight)
+    parts = (shift(down, -1), shift(up2, 2), shift(up, 1))
     own, up, far, down = call(first_sum_kernel, [ROWS, ROWS, CODED, CODED], own, *parts)
     far, down = shift(far, 4), shift(down, -4)
     up = shift(call(relay_kernel, CODED, up, far), 4)
-
-    words = state_table[row_states[0]]
-    bits = jnp.right_shift(words[:, :, None], jnp.arange(32, dtype=jnp.int32)) & 1
-    allowed = bits.astype(F32).reshape(8, N)
 
     outs = [ROWS, jax.ShapeDtypeStruct((32, 1, 384), F32)]
     logits, stats = call(stats_kernel, outs, own, down, up, allowed)

time: 93.4 us -> 91 us (0.974)
  waiting for transfers between devices: 25.9 us -> 24 us
  blocking collectives: 13.5 us -> 12.4 us
    all_to_all x2, waiting for transfers between devices: 15 us -> 13.2 us  [spread(): return lax.all_to_all(array, axis, 0, 0)]
    all_to_all x1, blocking collectives: 13.5 us -> 12.4 us  [spread(): return lax.all_to_all(array, axis, 0, 0)]
  transfers between devices with their start and end apart: 8 -> 8, of which waited for: 6 -> 6; matrix products, arithmetic and copies ran while one was open for 1% -> 2% of each run, Pallas kernels for 0% -> 0%
where the time goes in v5:
time: 91 us; the launch traced here: 90.5 us
  starting transfers between devices  45.2 us (50%)
  waiting for transfers between devices  24 us (26%)
  blocking collectives  12.4 us (14%)
  Pallas kernels  5.02 us (6%)
  local copies, waits for them, and re-layouts  1.75 us (2%)
  between operations  1.45 us (2%)
    ppermute x6, starting transfers between devices, shift(): return lax.ppermute(array, ('rows', 'vocab'), pairs)  30.9 us
    all_to_all x2, starting transfers between devices, spread(): return lax.all_to_all(array, axis, 0, 0)  14.3 us
    all_to_all x2, waiting for transfers between devices, spread(): return lax.all_to_all(array, axis, 0, 0)  13.2 us
    all_to_all x1, blocking collectives, spread(): return lax.all_to_all(array, axis, 0, 0)  12.4 us
    ppermute x6, waiting for transfers between devices, shift(): return lax.ppermute(array, ('rows', 'vocab'), pairs)  10.8 us
    pallas_call x1, Pallas kernels, product(): pl.pallas_call(product_kernel, in_specs=[pl.BlockSpec(memory_space=pltpu....  3.27 us
  transfers between devices with their start and end apart: 8, of which 6 were waited for; matrix products, arithmetic and copies ran while one was open for 2% of the time, Pallas kernels for 0%

profile of v5, /device:TPU:1, one launch (start us, length us, event | category | flops | bytes accessed | tf_op | source)
XLA Modules:
  0.0 90.5 jit_solution(340569156754249666)
XLA Ops:
  0.6 0.0 copy-start
  0.6 10.4 %all-to-all-start = ((bf16[32,16,128]{2,1,0:T(8,128)(2,1)}), bf16[32,16,128]{2,1,0:T(8,128)(2,1)S(1)}, u32[]{:S(2)}, u32[]{:S(2)}) async-start(bf16[32,16,128]{2,1,0:T(8,128)(2,1)} %bitcast.16), calls=%async_computation | async-start | bytes 262144 | tf_op jit(solution)/shard_map/all_to_all | solution.py:150
  11.1 0.7 fusion
  12.4 0.1 shift_right_arithmetic.23
  12.5 0.0 copy-done
  12.5 0.6 gather_fusion
  13.0 0.2 shift_right_arithmetic.20
  13.2 0.2 shift_right_arithmetic.21
  13.5 5.4 %all-to-all-done = bf16[32,16,128]{2,1,0:T(8,128)(2,1)S(1)} async-done(((bf16[32,16,128]{2,1,0:T(8,128)(2,1)}), bf16[32,16,128]{2,1,0:T(8,128)(2,1)S(1)}, u32[]{:S(2)}, u32[]{:S(2)}) %all-to-all-start) | async-done | bytes 131104 | tf_op jit(solution)/shard_map/all_to_all | solution.py:150
  18.9 0.7 broadcast_in_dim.15
  19.6 3.9 %all-to-all-start.1 = ((bf16[32,16,128]{2,1,0:T(8,128)(2,1)}), bf16[32,16,128]{2,1,0:T(8,128)(2,1)S(1)}, u32[]{:S(2)}, u32[]{:S(2)}) async-start(bf16[32,16,128]{2,1,0:T(8,128)(2,1)} %broadcast_in_dim.15), calls=%async_computation.1 | async-start | bytes 262144 | tf_op jit(solution)/shard_map/all_to_all | solution.py:150
  23.5 7.8 %all-to-all-done.1.x_ref = bf16[32,16,128]{2,1,0:T(8,128)(2,1)S(1)} async-done(((bf16[32,16,128]{2,1,0:T(8,128)(2,1)}), bf16[32,16,128]{2,1,0:T(8,128)(2,1)S(1)}, u32[]{:S(2)}, u32[]{:S(2)}) %all-to-all-start.1) | async-done | bytes 131104 | tf_op jit(solution)/shard_map/all_to_all | solution.py:150
  31.3 3.3 %shard_map.68 = (f32[32,4096]{1,0:T(8,128)S(1)}, s16[32,4224]{1,0:T(8,128)(2,1)S(1)}, s16[32,4224]{1,0:T(8,128)(2,1)S(1)}, s16[32,4224]{1,0:T(8,128)(2,1)S(1)}) custom-call(s32[1]{0:T(128)} %bitcast.z_ref, bf16[32,16,128]{2,1,0:T(8,128)(2,1)S(1)} %all-to-all-done.1.x_ref, bf16[512,4096]{1,0:T(8,128)(2,1)} %w_ref.1), custom_call_target="tpu_custom_call" | custom-call | flops 536870912 | bytes 6291456 | tf_op jit(solution)/shard_map/pallas_call | solution.py:65
  34.6 1.9 %collective-permute-start = (s16[32,4224]{1,0:T(8,128)(2,1)S(1)}, s16[32,4224]{1,0:T(8,128)(2,1)S(1)}, u32[]{:S(2)}, u32[]{:S(2)}) collective-permute-start(s16[32,4224]{1,0:T(8,128)(2,1)S(1)} %get-tuple-element.16), channel_id=1, source_target_pairs={{0,480},{1,33},{2,482},{3,35},{4,484},{5,37},{6,486},{7,39},{8,488... | collective-permute-start | bytes 811016 | tf_op jit(solution)/shard_map/ppermute | solution.py:160
  36.5 10.4 %collective-permute-start.1 = (s16[32,4224]{1,0:T(8,128)(2,1)S(1)}, s16[32,4224]{1,0:T(8,128)(2,1)S(1)}, u32[]{:S(2)}, u32[]{:S(2)}) collective-permute-start(s16[32,4224]{1,0:T(8,128)(2,1)S(1)} %get-tuple-element.17), channel_id=1, source_target_pairs={{0,64},{1,449},{2,66},{3,451},{4,68},{5,453},{6,70},{7,455},{8,72}... | collective-permute-start | bytes 811016 | tf_op jit(solution)/shard_map/ppermute | solution.py:160
  46.9 2.6 %collective-permute-start.2 = (s16[32,4224]{1,0:T(8,128)(2,1)S(1)}, s16[32,4224]{1,0:T(8,128)(2,1)S(1)}, u32[]{:S(2)}, u32[]{:S(2)}) collective-permute-start(s16[32,4224]{1,0:T(8,128)(2,1)S(1)} %get-tuple-element.18), channel_id=1, source_target_pairs={{0,32},{1,481},{2,34},{3,483},{4,36},{5,485},{6,38},{7,487},{8,40}... | collective-permute-start | bytes 811016 | tf_op jit(solution)/shard_map/ppermute | solution.py:160
  49.5 0.0 collective-permute-done.a_ref
  49.5 4.3 %collective-permute-done.1.b_ref = s16[32,4224]{1,0:T(8,128)(2,1)S(1)} collective-permute-done((s16[32,4224]{1,0:T(8,128)(2,1)S(1)}, s16[32,4224]{1,0:T(8,128)(2,1)S(1)}, u32[]{:S(2)}, u32[]{:S(2)}) %collective-permute-start.1) | collective-permute-done | bytes 270368 | tf_op jit(solution)/shard_map/ppermute | solution.py:160
  53.8 2.9 %collective-permute-done.2.c_ref = s16[32,4224]{1,0:T(8,128)(2,1)S(1)} collective-permute-done((s16[32,4224]{1,0:T(8,128)(2,1)S(1)}, s16[32,4224]{1,0:T(8,128)(2,1)S(1)}, u32[]{:S(2)}, u32[]{:S(2)}) %collective-permute-start.2) | collective-permute-done | bytes 270368 | tf_op jit(solution)/shard_map/ppermute | solution.py:160
  56.7 0.4 shard_map.69
  57.1 5.7 %collective-permute-start.4 = (s16[16,2176]{1,0:T(8,128)(2,1)S(1)}, s16[16,2176]{1,0:T(8,128)(2,1)S(1)}, u32[]{:S(2)}, u32[]{:S(2)}) collective-permute-start(s16[16,2176]{1,0:T(8,128)(2,1)S(1)} %get-tuple-element.22), channel_id=1, source_target_pairs={{0,128},{1,385},{2,130},{3,387},{4,132},{5,389},{6,134},{7,391},{8... | collective-permute-start | bytes 208904 | tf_op jit(solution)/shard_map/ppermute | solution.py:160
  62.8 3.5 %collective-permute-start.3 = (s16[16,2176]{1,0:T(8,128)(2,1)S(1)}, s16[16,2176]{1,0:T(8,128)(2,1)S(1)}, u32[]{:S(2)}, u32[]{:S(2)}) collective-permute-start(s16[16,2176]{1,0:T(8,128)(2,1)S(1)} %get-tuple-element.20), channel_id=1, source_target_pairs={{0,384},{1,129},{2,386},{3,131},{4,388},{5,133},{6,390},{7,135},{8... | collective-permute-start | bytes 208904 | tf_op jit(solution)/shard_map/ppermute | solution.py:160
  66.3 0.1 collective-permute-done.4.far_ref
  66.3 0.2 shard_map.70
  66.6 6.8 %collective-permute-start.5 = (s16[16,2176]{1,0:T(8,128)(2,1)S(1)}, s16[16,2176]{1,0:T(8,128)(2,1)S(1)}, u32[]{:S(2)}, u32[]{:S(2)}) collective-permute-start(s16[16,2176]{1,0:T(8,128)(2,1)S(1)} %shard_map.70), channel_id=1, source_target_pairs={{0,128},{1,385},{2,130},{3,387},{4,132},{5,389},{6,134},{7,391},{8... | collective-permute-start | bytes 208904 | tf_op jit(solution)/shard_map/ppermute | solution.py:160
  73.4 0.0 collective-permute-done.3.a_ref
  73.4 3.5 %collective-permute-done.5.b_ref = s16[16,2176]{1,0:T(8,128)(2,1)S(1)} collective-permute-done((s16[16,2176]{1,0:T(8,128)(2,1)S(1)}, s16[16,2176]{1,0:T(8,128)(2,1)S(1)}, u32[]{:S(2)}, u32[]{:S(2)}) %collective-permute-start.5) | collective-permute-done | bytes 69664 | tf_op jit(solution)/shard_map/ppermute | solution.py:160
  76.9 0.3 shard_map.71
  77.3 12.4 %all_to_all.15.stats_ref = f32[32,1,384]{2,1,0:T(1,128)S(1)} all-to-all(f32[32,1,384]{2,1,0:T(1,128)S(1)} %get-tuple-element.25), channel_id=1, replica_groups=mesh['rows'=16,'vocab'=32] {'vocab'}, dimensions={0} | all-to-all | bytes 98304 | tf_op jit(solution)/shard_map/all_to_all | solution.py:150
  89.7 0.8 shard_map.72
  (4 shorter events, 0.0 us)
Async XLA Ops:
  0.6 11.8 %copy-start = (s32[24,128]{1,0:T(8,128)S(1)}, s32[24,128]{1,0:T(8,128)}, u32[]{:S(2)}) copy-start(s32[24,128]{1,0:T(8,128)} %param.7) | copy-start | bytes 36868
  0.6 18.2 %all-to-all-start = ((bf16[32,16,128]{2,1,0:T(8,128)(2,1)}), bf16[32,16,128]{2,1,0:T(8,128)(2,1)S(1)}, u32[]{:S(2)}, u32[]{:S(2)}) async-start(bf16[32,16,128]{2,1,0:T(8,128)(2,1)} %bitcast.16), calls=%async_computation | async-start | bytes 262144 | tf_op jit(solution)/shard_map/all_to_all | solution.py:150
  19.6 11.7 %all-to-all-start.1 = ((bf16[32,16,128]{2,1,0:T(8,128)(2,1)}), bf16[32,16,128]{2,1,0:T(8,128)(2,1)S(1)}, u32[]{:S(2)}, u32[]{:S(2)}) async-start(bf16[32,16,128]{2,1,0:T(8,128)(2,1)} %broadcast_in_dim.15), calls=%async_computation.1 | async-start | bytes 262144 | tf_op jit(solution)/shard_map/all_to_all | solution.py:150
  34.6 15.0 %collective-permute-start = (s16[32,4224]{1,0:T(8,128)(2,1)S(1)}, s16[32,4224]{1,0:T(8,128)(2,1)S(1)}, u32[]{:S(2)}, u32[]{:S(2)}) collective-permute-start(s16[32,4224]{1,0:T(8,128)(2,1)S(1)} %get-tuple-element.16), channel_id=1, source_target_pairs={{0,480},{1,33},{2,482},{3,35},{4,484},{5,37},{6,486},{7,39},{8,488... | collective-permute-start | bytes 811016 | tf_op jit(solution)/shard_map/ppermute | solution.py:160
  36.5 17.3 %collective-permute-start.1 = (s16[32,4224]{1,0:T(8,128)(2,1)S(1)}, s16[32,4224]{1,0:T(8,128)(2,1)S(1)}, u32[]{:S(2)}, u32[]{:S(2)}) collective-permute-start(s16[32,4224]{1,0:T(8,128)(2,1)S(1)} %get-tuple-element.17), channel_id=1, source_target_pairs={{0,64},{1,449},{2,66},{3,451},{4,68},{5,453},{6,70},{7,455},{8,72}... | collective-permute-start | bytes 811016 | tf_op jit(solution)/shard_map/ppermute | solution.py:160
  46.9 9.8 %collective-permute-start.2 = (s16[32,4224]{1,0:T(8,128)(2,1)S(1)}, s16[32,4224]{1,0:T(8,128)(2,1)S(1)}, u32[]{:S(2)}, u32[]{:S(2)}) collective-permute-start(s16[32,4224]{1,0:T(8,128)(2,1)S(1)} %get-tuple-element.18), channel_id=1, source_target_pairs={{0,32},{1,481},{2,34},{3,483},{4,36},{5,485},{6,38},{7,487},{8,40}... | collective-permute-start | bytes 811016 | tf_op jit(solution)/shard_map/ppermute | solution.py:160
  57.1 9.3 %collective-permute-start.4 = (s16[16,2176]{1,0:T(8,128)(2,1)S(1)}, s16[16,2176]{1,0:T(8,128)(2,1)S(1)}, u32[]{:S(2)}, u32[]{:S(2)}) collective-permute-start(s16[16,2176]{1,0:T(8,128)(2,1)S(1)} %get-tuple-element.22), channel_id=1, source_target_pairs={{0,128},{1,385},{2,130},{3,387},{4,132},{5,389},{6,134},{7,391},{8... | collective-permute-start | bytes 208904 | tf_op jit(solution)/shard_map/ppermute | solution.py:160
  62.8 10.6 %collective-permute-start.3 = (s16[16,2176]{1,0:T(8,128)(2,1)S(1)}, s16[16,2176]{1,0:T(8,128)(2,1)S(1)}, u32[]{:S(2)}, u32[]{:S(2)}) collective-permute-start(s16[16,2176]{1,0:T(8,128)(2,1)S(1)} %get-tuple-element.20), channel_id=1, source_target_pairs={{0,384},{1,129},{2,386},{3,131},{4,388},{5,133},{6,390},{7,135},{8... | collective-permute-start | bytes 208904 | tf_op jit(solution)/shard_map/ppermute | solution.py:160
  66.6 10.4 %collective-permute-start.5 = (s16[16,2176]{1,0:T(8,128)(2,1)S(1)}, s16[16,2176]{1,0:T(8,128)(2,1)S(1)}, u32[]{:S(2)}, u32[]{:S(2)}) collective-permute-start(s16[16,2176]{1,0:T(8,128)(2,1)S(1)} %shard_map.70), channel_id=1, source_target_pairs={{0,128},{1,385},{2,130},{3,387},{4,132},{5,389},{6,134},{7,391},{8... | collective-permute-start | bytes 208904 | tf_op jit(solution)/shard_map/ppermute | solution.py:160

commit v6 on v5

--- a/solution.py
+++ b/solution.py
@@ -8,8 +8,9 @@
 N = 4096
 HALF = N // 2
 TAIL = 128
-TILES = 8
+TILES = 4
 WIDE = N // TILES
+AHEAD = 3
 F32 = jnp.float32
 I16 = jnp.int16
 
@@ -32,13 +33,37 @@
     return jnp.exp2(0.125 * to_f32(codes)[:, :1])
 
 
-def product_kernel(z_ref, x_ref, w_ref, own_ref, down_ref, up2_ref, up_ref, acc_ref, held_ref, sems):
-    def tile(t):
-        part = pl.ds(t * WIDE, WIDE)
-        return pltpu.make_async_copy(w_ref.at[:, part], held_ref.at[:, part], sems.at[t])
-
-    for t in range(TILES):
-        tile(t).start()
+def part(array, t):
+    return array.at[:, pl.ds(t * WIDE, WIDE)]
+
+
+def stage_kernel(w_ref, *refs):
+    copies = [pltpu.make_async_copy(part(w_ref, t), refs[t], refs[-1].at[t]) for t in range(AHEAD)]
+    for copy in copies:
+        copy.start()
+    for copy in copies:
+        copy.wait()
+
+
+def stage(w):
+    return pl.pallas_call(
+        stage_kernel,
+        in_specs=[pl.BlockSpec(memory_space=pl.ANY)],
+        out_specs=[pl.BlockSpec(memory_space=pl.ANY)] * AHEAD,
+        out_shape=[jax.ShapeDtypeStruct((w.shape[0], WIDE), w.dtype)] * AHEAD,
+        scratch_shapes=[pltpu.SemaphoreType.DMA((AHEAD,))],
+        compiler_params=pltpu.CompilerParams(vmem_limit_bytes=47 * 2**20),
+        cost_estimate=pl.CostEstimate(flops=0, bytes_accessed=2**23, transcendentals=0),
+    )(w)
+
+
+def product_kernel(z_ref, x_ref, w_ref, *refs):
+    staged, (own_ref, down_ref, up2_ref, up_ref, acc_ref, held_ref, sems) = refs[:AHEAD], refs[AHEAD:]
+    copies = [
+        pltpu.make_async_copy(part(w_ref, t), part(held_ref, t - AHEAD), sems.at[t - AHEAD]) for t in range(AHEAD, TILES)
+    ]
+    for copy in copies:
+        copy.start()
     x = x_ref[...].astype(F32).reshape(16, 2, 2, 8, 128)
     x = [x[:, h, t].reshape(128, 128) for h in range(2) for t in range(2)]
     x = jnp.concatenate(x, axis=1).astype(jnp.bfloat16)
@@ -49,10 +74,12 @@
     chosen = (source == 8 * piece + (i & 7)).astype(F32).astype(jnp.bfloat16)
     x = jnp.dot(chosen, x, preferred_element_type=F32).astype(jnp.bfloat16)
     for t in range(TILES):
-        tile(t).wait()
-        acc_ref[:, t * WIDE : (t + 1) * WIDE] = jnp.dot(
-            x, held_ref[:, t * WIDE : (t + 1) * WIDE], preferred_element_type=F32
-        )
+        if t < AHEAD:
+            tile = staged[t][...]
+        else:
+            copies[t - AHEAD].wait()
+            tile = held_ref[:, (t - AHEAD) * WIDE : (t - AHEAD + 1) * WIDE]
+        acc_ref[:, t * WIDE : (t + 1) * WIDE] = jnp.dot(x, tile, preferred_element_type=F32)
     own_ref[...] = acc_ref[:32]
     for ref, lo in ((up_ref, 32), (up2_ref, 64), (down_ref, 96)):
         q, k = encode(acc_ref[lo : lo + 32])
@@ -68,16 +95,17 @@
             pl.BlockSpec(memory_space=pltpu.SMEM),
             pl.BlockSpec(memory_space=pltpu.VMEM),
             pl.BlockSpec(memory_space=pl.ANY),
-        ],
+        ]
+        + [pl.BlockSpec(memory_space=pltpu.VMEM)] * AHEAD,
         out_shape=[jax.ShapeDtypeStruct(s, F32 if n == 0 else I16) for n, s in enumerate(outs)],
         scratch_shapes=[
             pltpu.VMEM((128, N), F32),
-            pltpu.VMEM(w.shape, w.dtype),
-            pltpu.SemaphoreType.DMA((TILES,)),
+            pltpu.VMEM((w.shape[0], (TILES - AHEAD) * WIDE), w.dtype),
+            pltpu.SemaphoreType.DMA((TILES - AHEAD,)),
         ],
-        compiler_params=pltpu.CompilerParams(vmem_limit_bytes=50 * 2**20),
+        compiler_params=pltpu.CompilerParams(vmem_limit_bytes=47 * 2**20),
         cost_estimate=pl.CostEstimate(flops=2 * 128 * 512 * N, bytes_accessed=6 * 2**20, transcendentals=0),
-    )(z, x, w)
+    )(z, x, w, *stage(w))
 
 
 def pack(ref, values):

time: 91 us -> 90.1 us (level)
  waiting for transfers between devices: 24 us -> 22.1 us
  Pallas kernels: 5.02 us -> 5.98 us
    all_to_all x2, waiting for transfers between devices: 13.2 us -> 11.3 us  [spread(): return lax.all_to_all(array, axis, 0, 0)]
    pallas_call x0 -> x1, Pallas kernels: none -> 1.89 us  [stage(): pl.pallas_call(stage_kernel, in_specs=[pl.BlockSpec(memory_space=pl.ANY)]...]
    pallas_call x1, Pallas kernels: 3.27 us -> 2.33 us  [product(): pl.pallas_call(product_kernel, in_specs=[pl.BlockSpec(memory_space=pltpu....]
  transfers between devices with their start and end apart: 8 -> 8, of which waited for: 6 -> 6; matrix products, arithmetic and copies ran while one was open for 2% -> 2% of each run, Pallas kernels for 0% -> 2%
where the time goes in v6:
time: 90.1 us; the launch traced here: 89.5 us
  starting transfers between devices  45.2 us (50%)
  waiting for transfers between devices  22.1 us (25%)
  blocking collectives  12.4 us (14%)
  Pallas kernels  5.98 us (7%)
  local copies, waits for them, and re-layouts  1.75 us (2%)
  between operations  1.47 us (2%)
    ppermute x6, starting transfers between devices, shift(): return lax.ppermute(array, ('rows', 'vocab'), pairs)  30.9 us
    all_to_all x2, starting transfers between devices, spread(): return lax.all_to_all(array, axis, 0, 0)  14.3 us
    all_to_all x1, blocking collectives, spread(): return lax.all_to_all(array, axis, 0, 0)  12.4 us
    all_to_all x2, waiting for transfers between devices, spread(): return lax.all_to_all(array, axis, 0, 0)  11.3 us
    ppermute x6, waiting for transfers between devices, shift(): return lax.ppermute(array, ('rows', 'vocab'), pairs)  10.8 us
    pallas_call x1, Pallas kernels, product(): pl.pallas_call(product_kernel, in_specs=[pl.BlockSpec(memory_space=pltpu....  2.33 us
    pallas_call x1, Pallas kernels, stage(): pl.pallas_call(stage_kernel, in_specs=[pl.BlockSpec(memory_space=pl.ANY)]...  1.89 us
  transfers between devices with their start and end apart: 8, of which 6 were waited for; matrix products, arithmetic and copies ran while one was open for 2% of the time, Pallas kernels for 2%

profile of v6, /device:TPU:1, one launch (start us, length us, event | category | flops | bytes accessed | tf_op | source)
XLA Modules:
  0.0 89.5 jit_solution(15589326650049111833)
XLA Ops:
  0.6 0.0 copy-start
  0.6 10.4 %all-to-all-start = ((bf16[32,16,128]{2,1,0:T(8,128)(2,1)}), bf16[32,16,128]{2,1,0:T(8,128)(2,1)S(1)}, u32[]{:S(2)}, u32[]{:S(2)}) async-start(bf16[32,16,128]{2,1,0:T(8,128)(2,1)} %bitcast.16), calls=%async_computation | async-start | bytes 262144 | tf_op jit(solution)/shard_map/all_to_all | solution.py:178
  11.1 0.7 fusion
  12.4 0.1 shift_right_arithmetic.23
  12.5 0.0 copy-done
  12.5 0.6 gather_fusion
  13.0 0.2 shift_right_arithmetic.20
  13.2 0.2 shift_right_arithmetic.21
  13.5 5.4 %all-to-all-done = bf16[32,16,128]{2,1,0:T(8,128)(2,1)S(1)} async-done(((bf16[32,16,128]{2,1,0:T(8,128)(2,1)}), bf16[32,16,128]{2,1,0:T(8,128)(2,1)S(1)}, u32[]{:S(2)}, u32[]{:S(2)}) %all-to-all-start) | async-done | bytes 131104 | tf_op jit(solution)/shard_map/all_to_all | solution.py:178
  18.9 0.7 broadcast_in_dim.15
  19.6 3.9 %all-to-all-start.1 = ((bf16[32,16,128]{2,1,0:T(8,128)(2,1)}), bf16[32,16,128]{2,1,0:T(8,128)(2,1)S(1)}, u32[]{:S(2)}, u32[]{:S(2)}) async-start(bf16[32,16,128]{2,1,0:T(8,128)(2,1)} %broadcast_in_dim.15), calls=%async_computation.1 | async-start | bytes 262144 | tf_op jit(solution)/shard_map/all_to_all | solution.py:178
  23.5 1.9 %shard_map.68 = (bf16[512,1024]{1,0:T(8,128)(2,1)S(1)}, bf16[512,1024]{1,0:T(8,128)(2,1)S(1)}, bf16[512,1024]{1,0:T(8,128)(2,1)S(1)}) custom-call(bf16[512,4096]{1,0:T(8,128)(2,1)} %w_ref.3), custom_call_target="tpu_custom_call" | custom-call | bytes 8388608 | tf_op jit(solution)/shard_map/pallas_call | solution.py:49
  25.4 5.9 %all-to-all-done.1.x_ref = bf16[32,16,128]{2,1,0:T(8,128)(2,1)S(1)} async-done(((bf16[32,16,128]{2,1,0:T(8,128)(2,1)}), bf16[32,16,128]{2,1,0:T(8,128)(2,1)S(1)}, u32[]{:S(2)}, u32[]{:S(2)}) %all-to-all-start.1) | async-done | bytes 131104 | tf_op jit(solution)/shard_map/all_to_all | solution.py:178
  31.3 2.3 %shard_map.69 = (f32[32,4096]{1,0:T(8,128)S(1)}, s16[32,4224]{1,0:T(8,128)(2,1)S(1)}, s16[32,4224]{1,0:T(8,128)(2,1)S(1)}, s16[32,4224]{1,0:T(8,128)(2,1)S(1)}) custom-call(s32[1]{0:T(128)} %bitcast.z_ref, bf16[32,16,128]{2,1,0:T(8,128)(2,1)S(1)} %all-to-all-done.1.x_ref, bf16[512,4096]{1,0:T(8,128)(2,1)} %w_ref.3, ...), custom_call_target="tpu_custom_call" | custom-call | flops 536870912 | bytes 6291456 | tf_op jit(solution)/shard_map/pallas_call | solution.py:92
  33.6 1.9 %collective-permute-start = (s16[32,4224]{1,0:T(8,128)(2,1)S(1)}, s16[32,4224]{1,0:T(8,128)(2,1)S(1)}, u32[]{:S(2)}, u32[]{:S(2)}) collective-permute-start(s16[32,4224]{1,0:T(8,128)(2,1)S(1)} %get-tuple-element.22), channel_id=1, source_target_pairs={{0,480},{1,33},{2,482},{3,35},{4,484},{5,37},{6,486},{7,39},{8,488... | collective-permute-start | bytes 811016 | tf_op jit(solution)/shard_map/ppermute | solution.py:188
  35.5 10.4 %collective-permute-start.1 = (s16[32,4224]{1,0:T(8,128)(2,1)S(1)}, s16[32,4224]{1,0:T(8,128)(2,1)S(1)}, u32[]{:S(2)}, u32[]{:S(2)}) collective-permute-start(s16[32,4224]{1,0:T(8,128)(2,1)S(1)} %get-tuple-element.23), channel_id=1, source_target_pairs={{0,64},{1,449},{2,66},{3,451},{4,68},{5,453},{6,70},{7,455},{8,72}... | collective-permute-start | bytes 811016 | tf_op jit(solution)/shard_map/ppermute | solution.py:188
  45.9 2.6 %collective-permute-start.2 = (s16[32,4224]{1,0:T(8,128)(2,1)S(1)}, s16[32,4224]{1,0:T(8,128)(2,1)S(1)}, u32[]{:S(2)}, u32[]{:S(2)}) collective-permute-start(s16[32,4224]{1,0:T(8,128)(2,1)S(1)} %get-tuple-element.24), channel_id=1, source_target_pairs={{0,32},{1,481},{2,34},{3,483},{4,36},{5,485},{6,38},{7,487},{8,40}... | collective-permute-start | bytes 811016 | tf_op jit(solution)/shard_map/ppermute | solution.py:188
  48.6 0.0 collective-permute-done.a_ref
  48.6 4.3 %collective-permute-done.1.b_ref = s16[32,4224]{1,0:T(8,128)(2,1)S(1)} collective-permute-done((s16[32,4224]{1,0:T(8,128)(2,1)S(1)}, s16[32,4224]{1,0:T(8,128)(2,1)S(1)}, u32[]{:S(2)}, u32[]{:S(2)}) %collective-permute-start.1) | collective-permute-done | bytes 270368 | tf_op jit(solution)/shard_map/ppermute | solution.py:188
  52.9 2.9 %collective-permute-done.2.c_ref = s16[32,4224]{1,0:T(8,128)(2,1)S(1)} collective-permute-done((s16[32,4224]{1,0:T(8,128)(2,1)S(1)}, s16[32,4224]{1,0:T(8,128)(2,1)S(1)}, u32[]{:S(2)}, u32[]{:S(2)}) %collective-permute-start.2) | collective-permute-done | bytes 270368 | tf_op jit(solution)/shard_map/ppermute | solution.py:188
  55.8 0.4 shard_map.70
  56.1 5.7 %collective-permute-start.4 = (s16[16,2176]{1,0:T(8,128)(2,1)S(1)}, s16[16,2176]{1,0:T(8,128)(2,1)S(1)}, u32[]{:S(2)}, u32[]{:S(2)}) collective-permute-start(s16[16,2176]{1,0:T(8,128)(2,1)S(1)} %get-tuple-element.28), channel_id=1, source_target_pairs={{0,128},{1,385},{2,130},{3,387},{4,132},{5,389},{6,134},{7,391},{8... | collective-permute-start | bytes 208904 | tf_op jit(solution)/shard_map/ppermute | solution.py:188
  61.8 3.5 %collective-permute-start.3 = (s16[16,2176]{1,0:T(8,128)(2,1)S(1)}, s16[16,2176]{1,0:T(8,128)(2,1)S(1)}, u32[]{:S(2)}, u32[]{:S(2)}) collective-permute-start(s16[16,2176]{1,0:T(8,128)(2,1)S(1)} %get-tuple-element.26), channel_id=1, source_target_pairs={{0,384},{1,129},{2,386},{3,131},{4,388},{5,133},{6,390},{7,135},{8... | collective-permute-start | bytes 208904 | tf_op jit(solution)/shard_map/ppermute | solution.py:188
  65.3 0.1 collective-permute-done.4.far_ref
  65.4 0.2 shard_map.71
  65.6 6.8 %collective-permute-start.5 = (s16[16,2176]{1,0:T(8,128)(2,1)S(1)}, s16[16,2176]{1,0:T(8,128)(2,1)S(1)}, u32[]{:S(2)}, u32[]{:S(2)}) collective-permute-start(s16[16,2176]{1,0:T(8,128)(2,1)S(1)} %shard_map.71), channel_id=1, source_target_pairs={{0,128},{1,385},{2,130},{3,387},{4,132},{5,389},{6,134},{7,391},{8... | collective-permute-start | bytes 208904 | tf_op jit(solution)/shard_map/ppermute | solution.py:188
  72.4 0.0 collective-permute-done.3.a_ref
  72.5 3.5 %collective-permute-done.5.b_ref = s16[16,2176]{1,0:T(8,128)(2,1)S(1)} collective-permute-done((s16[16,2176]{1,0:T(8,128)(2,1)S(1)}, s16[16,2176]{1,0:T(8,128)(2,1)S(1)}, u32[]{:S(2)}, u32[]{:S(2)}) %collective-permute-start.5) | collective-permute-done | bytes 69664 | tf_op jit(solution)/shard_map/ppermute | solution.py:188
  76.0 0.3 shard_map.72
  76.3 12.4 %all_to_all.15.stats_ref = f32[32,1,384]{2,1,0:T(1,128)S(1)} all-to-all(f32[32,1,384]{2,1,0:T(1,128)S(1)} %get-tuple-element.31), channel_id=1, replica_groups=mesh['rows'=16,'vocab'=32] {'vocab'}, dimensions={0} | all-to-all | bytes 98304 | tf_op jit(solution)/shard_map/all_to_all | solution.py:178
  88.7 0.8 shard_map.73
  (4 shorter events, 0.0 us)
Async XLA Ops:
  0.6 11.8 %copy-start = (s32[24,128]{1,0:T(8,128)S(1)}, s32[24,128]{1,0:T(8,128)}, u32[]{:S(2)}) copy-start(s32[24,128]{1,0:T(8,128)} %param.7) | copy-start | bytes 36868
  0.6 18.2 %all-to-all-start = ((bf16[32,16,128]{2,1,0:T(8,128)(2,1)}), bf16[32,16,128]{2,1,0:T(8,128)(2,1)S(1)}, u32[]{:S(2)}, u32[]{:S(2)}) async-start(bf16[32,16,128]{2,1,0:T(8,128)(2,1)} %bitcast.16), calls=%async_computation | async-start | bytes 262144 | tf_op jit(solution)/shard_map/all_to_all | solution.py:178
  19.6 11.7 %all-to-all-start.1 = ((bf16[32,16,128]{2,1,0:T(8,128)(2,1)}), bf16[32,16,128]{2,1,0:T(8,128)(2,1)S(1)}, u32[]{:S(2)}, u32[]{:S(2)}) async-start(bf16[32,16,128]{2,1,0:T(8,128)(2,1)} %broadcast_in_dim.15), calls=%async_computation.1 | async-start | bytes 262144 | tf_op jit(solution)/shard_map/all_to_all | solution.py:178
  33.6 15.0 %collective-permute-start = (s16[32,4224]{1,0:T(8,128)(2,1)S(1)}, s16[32,4224]{1,0:T(8,128)(2,1)S(1)}, u32[]{:S(2)}, u32[]{:S(2)}) collective-permute-start(s16[32,4224]{1,0:T(8,128)(2,1)S(1)} %get-tuple-element.22), channel_id=1, source_target_pairs={{0,480},{1,33},{2,482},{3,35},{4,484},{5,37},{6,486},{7,39},{8,488... | collective-permute-start | bytes 811016 | tf_op jit(solution)/shard_map/ppermute | solution.py:188
  35.5 17.3 %collective-permute-start.1 = (s16[32,4224]{1,0:T(8,128)(2,1)S(1)}, s16[32,4224]{1,0:T(8,128)(2,1)S(1)}, u32[]{:S(2)}, u32[]{:S(2)}) collective-permute-start(s16[32,4224]{1,0:T(8,128)(2,1)S(1)} %get-tuple-element.23), channel_id=1, source_target_pairs={{0,64},{1,449},{2,66},{3,451},{4,68},{5,453},{6,70},{7,455},{8,72}... | collective-permute-start | bytes 811016 | tf_op jit(solution)/shard_map/ppermute | solution.py:188
  45.9 9.8 %collective-permute-start.2 = (s16[32,4224]{1,0:T(8,128)(2,1)S(1)}, s16[32,4224]{1,0:T(8,128)(2,1)S(1)}, u32[]{:S(2)}, u32[]{:S(2)}) collective-permute-start(s16[32,4224]{1,0:T(8,128)(2,1)S(1)} %get-tuple-element.24), channel_id=1, source_target_pairs={{0,32},{1,481},{2,34},{3,483},{4,36},{5,485},{6,38},{7,487},{8,40}... | collective-permute-start | bytes 811016 | tf_op jit(solution)/shard_map/ppermute | solution.py:188
  56.1 9.3 %collective-permute-start.4 = (s16[16,2176]{1,0:T(8,128)(2,1)S(1)}, s16[16,2176]{1,0:T(8,128)(2,1)S(1)}, u32[]{:S(2)}, u32[]{:S(2)}) collective-permute-start(s16[16,2176]{1,0:T(8,128)(2,1)S(1)} %get-tuple-element.28), channel_id=1, source_target_pairs={{0,128},{1,385},{2,130},{3,387},{4,132},{5,389},{6,134},{7,391},{8... | collective-permute-start | bytes 208904 | tf_op jit(solution)/shard_map/ppermute | solution.py:188
  61.8 10.6 %collective-permute-start.3 = (s16[16,2176]{1,0:T(8,128)(2,1)S(1)}, s16[16,2176]{1,0:T(8,128)(2,1)S(1)}, u32[]{:S(2)}, u32[]{:S(2)}) collective-permute-start(s16[16,2176]{1,0:T(8,128)(2,1)S(1)} %get-tuple-element.26), channel_id=1, source_target_pairs={{0,384},{1,129},{2,386},{3,131},{4,388},{5,133},{6,390},{7,135},{8... | collective-permute-start | bytes 208904 | tf_op jit(solution)/shard_map/ppermute | solution.py:188
  65.6 10.3 %collective-permute-start.5 = (s16[16,2176]{1,0:T(8,128)(2,1)S(1)}, s16[16,2176]{1,0:T(8,128)(2,1)S(1)}, u32[]{:S(2)}, u32[]{:S(2)}) collective-permute-start(s16[16,2176]{1,0:T(8,128)(2,1)S(1)} %shard_map.71), channel_id=1, source_target_pairs={{0,128},{1,385},{2,130},{3,387},{4,132},{5,389},{6,134},{7,391},{8... | collective-permute-start | bytes 208904 | tf_op jit(solution)/shard_map/ppermute | solution.py:188

commit v7 on v6

--- a/solution.py
+++ b/solution.py
@@ -31,6 +31,19 @@
 
 def scale_of(codes):
     return jnp.exp2(0.125 * to_f32(codes)[:, :1])
+
+
+def choose_kernel(owner_ref, chunks_ref, out_ref):
+    out_ref[...] = jnp.broadcast_to(chunks_ref[pl.ds(owner_ref[0], 1)], out_ref.shape)
+
+
+def choose(owner, chunks):
+    return pl.pallas_call(
+        choose_kernel,
+        in_specs=[pl.BlockSpec(memory_space=pltpu.SMEM), pl.BlockSpec(memory_space=pltpu.VMEM)],
+        out_shape=jax.ShapeDtypeStruct(chunks.shape, chunks.dtype),
+        compiler_params=pltpu.CompilerParams(vmem_limit_bytes=24 * 2**20),
+    )(owner, chunks)
 
 
 def part(array, t):
@@ -154,19 +167,21 @@
     scaled = jnp.where(allowed, jnp.exp(logits - top), 0.0)
     total = jnp.sum(scaled, axis=1, keepdims=True)
     weighted = jnp.sum(jnp.where(allowed, scaled * logits, 0.0), axis=1, keepdims=True)
-    own_lane = lax.broadcasted_iota(jnp.int32, (8, 128), 1) == lax.broadcasted_iota(jnp.int32, (8, 128), 0)
+    lane = lax.broadcasted_iota(jnp.int32, (8, 128), 1)
+    row = lax.broadcasted_iota(jnp.int32, (8, 128), 0)
+    tile = jnp.zeros((8, 128), F32)
     for n, column in enumerate((top, total, weighted)):
-        row = jnp.sum(jnp.where(own_lane, column, 0.0), axis=0, keepdims=True)
-        stats_ref[:, :, 128 * n : 128 * n + 128] = jnp.broadcast_to(row[None], (32, 1, 128))
+        tile = jnp.where(lane == row + 8 * n, column, tile)
+    stats_ref[...] = jnp.broadcast_to(jnp.sum(tile, axis=0, keepdims=True)[None], stats_ref.shape)
 
 
 def finish_kernel(logits_ref, allowed_ref, stats_ref, log_probs_ref, entropy_ref):
-    top = stats_ref[:, :, :128]
+    lane = lax.broadcasted_iota(jnp.int32, (1, 128), 1)
+    top = stats_ref[...]
     row_max = jnp.max(top, axis=0)
-    factor = jnp.exp(top - row_max[None])
-    lane = lax.broadcasted_iota(jnp.int32, (1, 128), 1)
-    total = jnp.where(lane < 8, jnp.sum(stats_ref[:, :, 128:256] * factor, axis=0), 1.0)
-    weighted = jnp.sum(stats_ref[:, :, 256:] * factor, axis=0)
+    factor = jnp.where(lane < 8, jnp.exp(top - row_max[None]), 0.0)
+    total = jnp.where(lane < 8, jnp.sum(pltpu.roll(top, 120, 2) * factor, axis=0), 1.0)
+    weighted = jnp.sum(pltpu.roll(top, 112, 2) * factor, axis=0)
     log_norm = row_max + jnp.log(total)
     entropy_ref[...] = (log_norm - weighted / total)[:, :8]
     own_lane = lax.broadcasted_iota(jnp.int32, (8, 128), 1) == lax.broadcasted_iota(jnp.int32, (8, 128), 0)
@@ -191,8 +206,8 @@
 def shards(hidden_held, head_weight, state_table, row_states, owner):
     z = (lax.axis_index("rows") + 16 * (lax.axis_index("vocab") & 1)).astype(jnp.int32)[None]
     chunks = hidden_held[0, 0].reshape(16, 8, 4, 128).transpose(0, 2, 1, 3).reshape(32, 16, 128)
-    mine = lax.dynamic_index_in_dim(spread(chunks, "vocab"), owner[0], 0, keepdims=True)
-    x = spread(jnp.broadcast_to(mine, (32, 16, 128)), "vocab")
+    mine = choose(owner, spread(chunks, "vocab"))
+    x = spread(mine, "vocab")
     words = state_table[row_states[0]]
     bits = jnp.right_shift(words[:, :, None], jnp.arange(32, dtype=jnp.int32)) & 1
     allowed = bits.astype(F32).reshape(8, N)
@@ -205,7 +220,7 @@
     far, down = shift(far, 4), shift(down, -4)
     up = shift(call(relay_kernel, CODED, up, far), 4)
 
-    outs = [ROWS, jax.ShapeDtypeStruct((32, 1, 384), F32)]
+    outs = [ROWS, jax.ShapeDtypeStruct((32, 1, 128), F32)]
     logits, stats = call(stats_kernel, outs, own, down, up, allowed)
     stats = spread(stats, "vocab")
     outs = [jax.ShapeDtypeStruct((1, 8, N), F32), jax.ShapeDtypeStruct((1, 8), F32)]

time: 90.1 us -> 89.7 us (level)
  no operation moved by 1% of the time
where the time goes in v7:
time: 89.7 us; the launch traced here: 89.2 us
  starting transfers between devices  45.2 us (50%)
  waiting for transfers between devices  22.1 us (25%)
  blocking collectives  12 us (13%)
  Pallas kernels  6.7 us (7%)
  between operations  1.46 us (2%)
  local copies, waits for them, and re-layouts  1.08 us (1%)
    ppermute x6, starting transfers between devices, shift(): return lax.ppermute(array, ('rows', 'vocab'), pairs)  30.9 us
    all_to_all x2, starting transfers between devices, spread(): return lax.all_to_all(array, axis, 0, 0)  14.3 us
    all_to_all x1, blocking collectives, spread(): return lax.all_to_all(array, axis, 0, 0)  12 us
    all_to_all x2, waiting for transfers between devices, spread(): return lax.all_to_all(array, axis, 0, 0)  11.3 us
    ppermute x6, waiting for transfers between devices, shift(): return lax.ppermute(array, ('rows', 'vocab'), pairs)  10.8 us
    pallas_call x1, Pallas kernels, product(): pl.pallas_call(product_kernel, in_specs=[pl.BlockSpec(memory_space=pltpu....  2.33 us
    pallas_call x1, Pallas kernels, stage(): pl.pallas_call(stage_kernel, in_specs=[pl.BlockSpec(memory_space=pl.ANY)]...  1.89 us
    pallas_call x4, Pallas kernels, call(): pl.pallas_call(kernel, out_shape=outs, compiler_params=pltpu.CompilerPara...  1.8 us
  transfers between devices with their start and end apart: 8, of which 6 were waited for; matrix products, arithmetic and copies ran while one was open for 2% of the time, Pallas kernels for 2%

profile of v7, /device:TPU:1, one launch (start us, length us, event | category | flops | bytes accessed | tf_op | source)
XLA Modules:
  0.0 89.2 jit_solution(11797786806193779387)
XLA Ops:
  0.6 0.0 copy-start
  0.6 10.4 %all-to-all-start = ((bf16[32,16,128]{2,1,0:T(8,128)(2,1)}), bf16[32,16,128]{2,1,0:T(8,128)(2,1)S(1)}, u32[]{:S(2)}, u32[]{:S(2)}) async-start(bf16[32,16,128]{2,1,0:T(8,128)(2,1)} %bitcast.10), calls=%async_computation | async-start | bytes 262144 | tf_op jit(solution)/shard_map/all_to_all | solution.py:193
  11.1 0.7 fusion
  12.4 0.1 shift_right_arithmetic.23
  12.5 0.0 copy-done
  12.5 0.6 gather_fusion
  13.0 0.2 shift_right_arithmetic.20
  13.2 0.2 shift_right_arithmetic.21
  13.5 5.4 %all-to-all-done.chunks_ref = bf16[32,16,128]{2,1,0:T(8,128)(2,1)S(1)} async-done(((bf16[32,16,128]{2,1,0:T(8,128)(2,1)}), bf16[32,16,128]{2,1,0:T(8,128)(2,1)S(1)}, u32[]{:S(2)}, u32[]{:S(2)}) %all-to-all-start) | async-done | bytes 131104 | tf_op jit(solution)/shard_map/all_to_all | solution.py:193
  18.9 0.7 shard_map.68
  19.5 3.9 %all-to-all-start.1 = ((bf16[32,16,128]{2,1,0:T(8,128)(2,1)}), bf16[32,16,128]{2,1,0:T(8,128)(2,1)S(1)}, u32[]{:S(2)}, u32[]{:S(2)}) async-start(bf16[32,16,128]{2,1,0:T(8,128)(2,1)} %shard_map.68), calls=%async_computation.1 | async-start | bytes 262144 | tf_op jit(solution)/shard_map/all_to_all | solution.py:193
  23.5 1.9 %shard_map.69 = (bf16[512,1024]{1,0:T(8,128)(2,1)S(1)}, bf16[512,1024]{1,0:T(8,128)(2,1)S(1)}, bf16[512,1024]{1,0:T(8,128)(2,1)S(1)}) custom-call(bf16[512,4096]{1,0:T(8,128)(2,1)} %w_ref.3), custom_call_target="tpu_custom_call" | custom-call | bytes 8388608 | tf_op jit(solution)/shard_map/pallas_call | solution.py:62
  25.4 5.9 %all-to-all-done.1.x_ref = bf16[32,16,128]{2,1,0:T(8,128)(2,1)S(1)} async-done(((bf16[32,16,128]{2,1,0:T(8,128)(2,1)}), bf16[32,16,128]{2,1,0:T(8,128)(2,1)S(1)}, u32[]{:S(2)}, u32[]{:S(2)}) %all-to-all-start.1) | async-done | bytes 131104 | tf_op jit(solution)/shard_map/all_to_all | solution.py:193
  31.3 2.3 %shard_map.70 = (f32[32,4096]{1,0:T(8,128)S(1)}, s16[32,4224]{1,0:T(8,128)(2,1)S(1)}, s16[32,4224]{1,0:T(8,128)(2,1)S(1)}, s16[32,4224]{1,0:T(8,128)(2,1)S(1)}) custom-call(s32[1]{0:T(128)} %bitcast.z_ref, bf16[32,16,128]{2,1,0:T(8,128)(2,1)S(1)} %all-to-all-done.1.x_ref, bf16[512,4096]{1,0:T(8,128)(2,1)} %w_ref.3, ...), custom_call_target="tpu_custom_call" | custom-call | flops 536870912 | bytes 6291456 | tf_op jit(solution)/shard_map/pallas_call | solution.py:105
  33.6 1.9 %collective-permute-start = (s16[32,4224]{1,0:T(8,128)(2,1)S(1)}, s16[32,4224]{1,0:T(8,128)(2,1)S(1)}, u32[]{:S(2)}, u32[]{:S(2)}) collective-permute-start(s16[32,4224]{1,0:T(8,128)(2,1)S(1)} %get-tuple-element.22), channel_id=1, source_target_pairs={{0,480},{1,33},{2,482},{3,35},{4,484},{5,37},{6,486},{7,39},{8,488... | collective-permute-start | bytes 811016 | tf_op jit(solution)/shard_map/ppermute | solution.py:203
  35.5 10.4 %collective-permute-start.1 = (s16[32,4224]{1,0:T(8,128)(2,1)S(1)}, s16[32,4224]{1,0:T(8,128)(2,1)S(1)}, u32[]{:S(2)}, u32[]{:S(2)}) collective-permute-start(s16[32,4224]{1,0:T(8,128)(2,1)S(1)} %get-tuple-element.23), channel_id=1, source_target_pairs={{0,64},{1,449},{2,66},{3,451},{4,68},{5,453},{6,70},{7,455},{8,72}... | collective-permute-start | bytes 811016 | tf_op jit(solution)/shard_map/ppermute | solution.py:203
  45.9 2.6 %collective-permute-start.2 = (s16[32,4224]{1,0:T(8,128)(2,1)S(1)}, s16[32,4224]{1,0:T(8,128)(2,1)S(1)}, u32[]{:S(2)}, u32[]{:S(2)}) collective-permute-start(s16[32,4224]{1,0:T(8,128)(2,1)S(1)} %get-tuple-element.24), channel_id=1, source_target_pairs={{0,32},{1,481},{2,34},{3,483},{4,36},{5,485},{6,38},{7,487},{8,40}... | collective-permute-start | bytes 811016 | tf_op jit(solution)/shard_map/ppermute | solution.py:203
  48.6 0.0 collective-permute-done.a_ref
  48.6 4.3 %collective-permute-done.1.b_ref = s16[32,4224]{1,0:T(8,128)(2,1)S(1)} collective-permute-done((s16[32,4224]{1,0:T(8,128)(2,1)S(1)}, s16[32,4224]{1,0:T(8,128)(2,1)S(1)}, u32[]{:S(2)}, u32[]{:S(2)}) %collective-permute-start.1) | collective-permute-done | bytes 270368 | tf_op jit(solution)/shard_map/ppermute | solution.py:203
  52.9 2.9 %collective-permute-done.2.c_ref = s16[32,4224]{1,0:T(8,128)(2,1)S(1)} collective-permute-done((s16[32,4224]{1,0:T(8,128)(2,1)S(1)}, s16[32,4224]{1,0:T(8,128)(2,1)S(1)}, u32[]{:S(2)}, u32[]{:S(2)}) %collective-permute-start.2) | collective-permute-done | bytes 270368 | tf_op jit(solution)/shard_map/ppermute | solution.py:203
  55.8 0.4 shard_map.71
  56.1 5.7 %collective-permute-start.4 = (s16[16,2176]{1,0:T(8,128)(2,1)S(1)}, s16[16,2176]{1,0:T(8,128)(2,1)S(1)}, u32[]{:S(2)}, u32[]{:S(2)}) collective-permute-start(s16[16,2176]{1,0:T(8,128)(2,1)S(1)} %get-tuple-element.28), channel_id=1, source_target_pairs={{0,128},{1,385},{2,130},{3,387},{4,132},{5,389},{6,134},{7,391},{8... | collective-permute-start | bytes 208904 | tf_op jit(solution)/shard_map/ppermute | solution.py:203
  61.8 3.5 %collective-permute-start.3 = (s16[16,2176]{1,0:T(8,128)(2,1)S(1)}, s16[16,2176]{1,0:T(8,128)(2,1)S(1)}, u32[]{:S(2)}, u32[]{:S(2)}) collective-permute-start(s16[16,2176]{1,0:T(8,128)(2,1)S(1)} %get-tuple-element.26), channel_id=1, source_target_pairs={{0,384},{1,129},{2,386},{3,131},{4,388},{5,133},{6,390},{7,135},{8... | collective-permute-start | bytes 208904 | tf_op jit(solution)/shard_map/ppermute | solution.py:203
  65.3 0.1 collective-permute-done.4.far_ref
  65.4 0.2 shard_map.72
  65.6 6.8 %collective-permute-start.5 = (s16[16,2176]{1,0:T(8,128)(2,1)S(1)}, s16[16,2176]{1,0:T(8,128)(2,1)S(1)}, u32[]{:S(2)}, u32[]{:S(2)}) collective-permute-start(s16[16,2176]{1,0:T(8,128)(2,1)S(1)} %shard_map.72), channel_id=1, source_target_pairs={{0,128},{1,385},{2,130},{3,387},{4,132},{5,389},{6,134},{7,391},{8... | collective-permute-start | bytes 208904 | tf_op jit(solution)/shard_map/ppermute | solution.py:203
  72.4 0.0 collective-permute-done.3.a_ref
  72.5 3.5 %collective-permute-done.5.b_ref = s16[16,2176]{1,0:T(8,128)(2,1)S(1)} collective-permute-done((s16[16,2176]{1,0:T(8,128)(2,1)S(1)}, s16[16,2176]{1,0:T(8,128)(2,1)S(1)}, u32[]{:S(2)}, u32[]{:S(2)}) %collective-permute-start.5) | collective-permute-done | bytes 69664 | tf_op jit(solution)/shard_map/ppermute | solution.py:203
  76.0 0.3 shard_map.73
  76.3 12.0 %all_to_all.15.stats_ref = f32[32,1,128]{2,1,0:T(1,128)S(1)} all-to-all(f32[32,1,128]{2,1,0:T(1,128)S(1)} %get-tuple-element.31), channel_id=1, replica_groups=mesh['rows'=16,'vocab'=32] {'vocab'}, dimensions={0} | all-to-all | bytes 32768 | tf_op jit(solution)/shard_map/all_to_all | solution.py:193
  88.3 0.9 shard_map.74
  (3 shorter events, 0.0 us)
Async XLA Ops:
  0.6 11.8 %copy-start = (s32[24,128]{1,0:T(8,128)S(1)}, s32[24,128]{1,0:T(8,128)}, u32[]{:S(2)}) copy-start(s32[24,128]{1,0:T(8,128)} %param.7) | copy-start | bytes 36868
  0.6 18.2 %all-to-all-start = ((bf16[32,16,128]{2,1,0:T(8,128)(2,1)}), bf16[32,16,128]{2,1,0:T(8,128)(2,1)S(1)}, u32[]{:S(2)}, u32[]{:S(2)}) async-start(bf16[32,16,128]{2,1,0:T(8,128)(2,1)} %bitcast.10), calls=%async_computation | async-start | bytes 262144 | tf_op jit(solution)/shard_map/all_to_all | solution.py:193
  19.5 11.7 %all-to-all-start.1 = ((bf16[32,16,128]{2,1,0:T(8,128)(2,1)}), bf16[32,16,128]{2,1,0:T(8,128)(2,1)S(1)}, u32[]{:S(2)}, u32[]{:S(2)}) async-start(bf16[32,16,128]{2,1,0:T(8,128)(2,1)} %shard_map.68), calls=%async_computation.1 | async-start | bytes 262144 | tf_op jit(solution)/shard_map/all_to_all | solution.py:193
  33.6 15.0 %collective-permute-start = (s16[32,4224]{1,0:T(8,128)(2,1)S(1)}, s16[32,4224]{1,0:T(8,128)(2,1)S(1)}, u32[]{:S(2)}, u32[]{:S(2)}) collective-permute-start(s16[32,4224]{1,0:T(8,128)(2,1)S(1)} %get-tuple-element.22), channel_id=1, source_target_pairs={{0,480},{1,33},{2,482},{3,35},{4,484},{5,37},{6,486},{7,39},{8,488... | collective-permute-start | bytes 811016 | tf_op jit(solution)/shard_map/ppermute | solution.py:203
  35.5 17.3 %collective-permute-start.1 = (s16[32,4224]{1,0:T(8,128)(2,1)S(1)}, s16[32,4224]{1,0:T(8,128)(2,1)S(1)}, u32[]{:S(2)}, u32[]{:S(2)}) collective-permute-start(s16[32,4224]{1,0:T(8,128)(2,1)S(1)} %get-tuple-element.23), channel_id=1, source_target_pairs={{0,64},{1,449},{2,66},{3,451},{4,68},{5,453},{6,70},{7,455},{8,72}... | collective-permute-start | bytes 811016 | tf_op jit(solution)/shard_map/ppermute | solution.py:203
  45.9 9.8 %collective-permute-start.2 = (s16[32,4224]{1,0:T(8,128)(2,1)S(1)}, s16[32,4224]{1,0:T(8,128)(2,1)S(1)}, u32[]{:S(2)}, u32[]{:S(2)}) collective-permute-start(s16[32,4224]{1,0:T(8,128)(2,1)S(1)} %get-tuple-element.24), channel_id=1, source_target_pairs={{0,32},{1,481},{2,34},{3,483},{4,36},{5,485},{6,38},{7,487},{8,40}... | collective-permute-start | bytes 811016 | tf_op jit(solution)/shard_map/ppermute | solution.py:203
  56.1 9.3 %collective-permute-start.4 = (s16[16,2176]{1,0:T(8,128)(2,1)S(1)}, s16[16,2176]{1,0:T(8,128)(2,1)S(1)}, u32[]{:S(2)}, u32[]{:S(2)}) collective-permute-start(s16[16,2176]{1,0:T(8,128)(2,1)S(1)} %get-tuple-element.28), channel_id=1, source_target_pairs={{0,128},{1,385},{2,130},{3,387},{4,132},{5,389},{6,134},{7,391},{8... | collective-permute-start | bytes 208904 | tf_op jit(solution)/shard_map/ppermute | solution.py:203
  61.8 10.6 %collective-permute-start.3 = (s16[16,2176]{1,0:T(8,128)(2,1)S(1)}, s16[16,2176]{1,0:T(8,128)(2,1)S(1)}, u32[]{:S(2)}, u32[]{:S(2)}) collective-permute-start(s16[16,2176]{1,0:T(8,128)(2,1)S(1)} %get-tuple-element.26), channel_id=1, source_target_pairs={{0,384},{1,129},{2,386},{3,131},{4,388},{5,133},{6,390},{7,135},{8... | collective-permute-start | bytes 208904 | tf_op jit(solution)/shard_map/ppermute | solution.py:203
  65.6 10.4 %collective-permute-start.5 = (s16[16,2176]{1,0:T(8,128)(2,1)S(1)}, s16[16,2176]{1,0:T(8,128)(2,1)S(1)}, u32[]{:S(2)}, u32[]{:S(2)}) collective-permute-start(s16[16,2176]{1,0:T(8,128)(2,1)S(1)} %shard_map.72), channel_id=1, source_target_pairs={{0,128},{1,385},{2,130},{3,387},{4,132},{5,389},{6,134},{7,391},{8... | collective-permute-start | bytes 208904 | tf_op jit(solution)/shard_map/ppermute | solution.py:203

commit v8 on v7

--- a/solution.py
+++ b/solution.py
@@ -6,7 +6,6 @@
 from jax.sharding import PartitionSpec as P
 
 N = 4096
-HALF = N // 2
 TAIL = 128
 TILES = 4
 WIDE = N // TILES
@@ -123,13 +122,12 @@
 
 def pack(ref, values):
     q, k = encode(values)
-    ref[:, :HALF] = to_i16(jnp.concatenate([q[:, :HALF], q[:, HALF:]], axis=0))
-    ref[:, HALF:] = to_i16(jnp.broadcast_to(jnp.concatenate([k, k], axis=0), (16, TAIL)))
+    ref[:, :N] = to_i16(q)
+    ref[:, N:] = to_i16(jnp.broadcast_to(k, (8, TAIL)))
 
 
 def unpack(ref):
-    part = to_f32(ref[:, :HALF]) * scale_of(ref[:, HALF:])
-    return jnp.concatenate([part[:8], part[8:]], axis=1)
+    return to_f32(ref[:, :N]) * scale_of(ref[:, N:])
 
 
 def first_sum_kernel(own_ref, a_ref, b_ref, c_ref, keep_ref, up_ref, far_ref, down_ref):
@@ -147,7 +145,7 @@
 
 
 ROWS = jax.ShapeDtypeStruct((8, N), F32)
-CODED = jax.ShapeDtypeStruct((16, HALF + TAIL), I16)
+CODED = jax.ShapeDtypeStruct((8, N + TAIL), I16)
 
 
 def call(kernel, outs, *arrays):

time: 89.7 us -> 89.6 us (level)
  transfers between devices with their start and end apart: 8 -> 8, of which waited for: 6 -> 5; matrix products, arithmetic and copies ran while one was open for 2% -> 2% of each run, Pallas kernels for 2% -> 2%
where the time goes in v8:
time: 89.6 us; the launch traced here: 89.1 us
  starting transfers between devices  45.2 us (50%)
  waiting for transfers between devices  22 us (25%)
  blocking collectives  12 us (13%)
  Pallas kernels  6.63 us (7%)
  between operations  1.47 us (2%)
  local copies, waits for them, and re-layouts  1.08 us (1%)
    ppermute x6, starting transfers between devices, shift(): return lax.ppermute(array, ('rows', 'vocab'), pairs)  30.9 us
    all_to_all x2, starting transfers between devices, spread(): return lax.all_to_all(array, axis, 0, 0)  14.3 us
    all_to_all x1, blocking collectives, spread(): return lax.all_to_all(array, axis, 0, 0)  12 us
    all_to_all x2, waiting for transfers between devices, spread(): return lax.all_to_all(array, axis, 0, 0)  11.3 us
    ppermute x6, waiting for transfers between devices, shift(): return lax.ppermute(array, ('rows', 'vocab'), pairs)  10.7 us
    pallas_call x1, Pallas kernels, product(): pl.pallas_call(product_kernel, in_specs=[pl.BlockSpec(memory_space=pltpu....  2.33 us
    pallas_call x1, Pallas kernels, stage(): pl.pallas_call(stage_kernel, in_specs=[pl.BlockSpec(memory_space=pl.ANY)]...  1.89 us
  transfers between devices with their start and end apart: 8, of which 5 were waited for; matrix products, arithmetic and copies ran while one was open for 2% of the time, Pallas kernels for 2%

profile of v8, /device:TPU:1, one launch (start us, length us, event | category | flops | bytes accessed | tf_op | source)
XLA Modules:
  0.0 89.1 jit_solution(11690040579478083982)
XLA Ops:
  0.6 0.0 copy-start
  0.6 10.4 %all-to-all-start = ((bf16[32,16,128]{2,1,0:T(8,128)(2,1)}), bf16[32,16,128]{2,1,0:T(8,128)(2,1)S(1)}, u32[]{:S(2)}, u32[]{:S(2)}) async-start(bf16[32,16,128]{2,1,0:T(8,128)(2,1)} %bitcast.10), calls=%async_computation | async-start | bytes 262144 | tf_op jit(solution)/shard_map/all_to_all | solution.py:191
  11.1 0.7 fusion
  12.4 0.1 shift_right_arithmetic.23
  12.5 0.0 copy-done
  12.5 0.6 gather_fusion
  13.0 0.2 shift_right_arithmetic.20
  13.2 0.2 shift_right_arithmetic.21
  13.5 5.4 %all-to-all-done.chunks_ref = bf16[32,16,128]{2,1,0:T(8,128)(2,1)S(1)} async-done(((bf16[32,16,128]{2,1,0:T(8,128)(2,1)}), bf16[32,16,128]{2,1,0:T(8,128)(2,1)S(1)}, u32[]{:S(2)}, u32[]{:S(2)}) %all-to-all-start) | async-done | bytes 131104 | tf_op jit(solution)/shard_map/all_to_all | solution.py:191
  18.9 0.7 shard_map.68
  19.5 3.9 %all-to-all-start.1 = ((bf16[32,16,128]{2,1,0:T(8,128)(2,1)}), bf16[32,16,128]{2,1,0:T(8,128)(2,1)S(1)}, u32[]{:S(2)}, u32[]{:S(2)}) async-start(bf16[32,16,128]{2,1,0:T(8,128)(2,1)} %shard_map.68), calls=%async_computation.1 | async-start | bytes 262144 | tf_op jit(solution)/shard_map/all_to_all | solution.py:191
  23.5 1.9 %shard_map.69 = (bf16[512,1024]{1,0:T(8,128)(2,1)S(1)}, bf16[512,1024]{1,0:T(8,128)(2,1)S(1)}, bf16[512,1024]{1,0:T(8,128)(2,1)S(1)}) custom-call(bf16[512,4096]{1,0:T(8,128)(2,1)} %w_ref.3), custom_call_target="tpu_custom_call" | custom-call | bytes 8388608 | tf_op jit(solution)/shard_map/pallas_call | solution.py:61
  25.4 5.9 %all-to-all-done.1.x_ref = bf16[32,16,128]{2,1,0:T(8,128)(2,1)S(1)} async-done(((bf16[32,16,128]{2,1,0:T(8,128)(2,1)}), bf16[32,16,128]{2,1,0:T(8,128)(2,1)S(1)}, u32[]{:S(2)}, u32[]{:S(2)}) %all-to-all-start.1) | async-done | bytes 131104 | tf_op jit(solution)/shard_map/all_to_all | solution.py:191
  31.3 2.3 %shard_map.70 = (f32[32,4096]{1,0:T(8,128)S(1)}, s16[32,4224]{1,0:T(8,128)(2,1)S(1)}, s16[32,4224]{1,0:T(8,128)(2,1)S(1)}, s16[32,4224]{1,0:T(8,128)(2,1)S(1)}) custom-call(s32[1]{0:T(128)} %bitcast.z_ref, bf16[32,16,128]{2,1,0:T(8,128)(2,1)S(1)} %all-to-all-done.1.x_ref, bf16[512,4096]{1,0:T(8,128)(2,1)} %w_ref.3, ...), custom_call_target="tpu_custom_call" | custom-call | flops 536870912 | bytes 6291456 | tf_op jit(solution)/shard_map/pallas_call | solution.py:104
  33.6 1.9 %collective-permute-start = (s16[32,4224]{1,0:T(8,128)(2,1)S(1)}, s16[32,4224]{1,0:T(8,128)(2,1)S(1)}, u32[]{:S(2)}, u32[]{:S(2)}) collective-permute-start(s16[32,4224]{1,0:T(8,128)(2,1)S(1)} %get-tuple-element.22), channel_id=1, source_target_pairs={{0,480},{1,33},{2,482},{3,35},{4,484},{5,37},{6,486},{7,39},{8,488... | collective-permute-start | bytes 811016 | tf_op jit(solution)/shard_map/ppermute | solution.py:201
  35.5 10.4 %collective-permute-start.1 = (s16[32,4224]{1,0:T(8,128)(2,1)S(1)}, s16[32,4224]{1,0:T(8,128)(2,1)S(1)}, u32[]{:S(2)}, u32[]{:S(2)}) collective-permute-start(s16[32,4224]{1,0:T(8,128)(2,1)S(1)} %get-tuple-element.23), channel_id=1, source_target_pairs={{0,64},{1,449},{2,66},{3,451},{4,68},{5,453},{6,70},{7,455},{8,72}... | collective-permute-start | bytes 811016 | tf_op jit(solution)/shard_map/ppermute | solution.py:201
  45.9 2.6 %collective-permute-start.2 = (s16[32,4224]{1,0:T(8,128)(2,1)S(1)}, s16[32,4224]{1,0:T(8,128)(2,1)S(1)}, u32[]{:S(2)}, u32[]{:S(2)}) collective-permute-start(s16[32,4224]{1,0:T(8,128)(2,1)S(1)} %get-tuple-element.24), channel_id=1, source_target_pairs={{0,32},{1,481},{2,34},{3,483},{4,36},{5,485},{6,38},{7,487},{8,40}... | collective-permute-start | bytes 811016 | tf_op jit(solution)/shard_map/ppermute | solution.py:201
  48.6 0.0 collective-permute-done.a_ref
  48.6 4.3 %collective-permute-done.1.b_ref = s16[32,4224]{1,0:T(8,128)(2,1)S(1)} collective-permute-done((s16[32,4224]{1,0:T(8,128)(2,1)S(1)}, s16[32,4224]{1,0:T(8,128)(2,1)S(1)}, u32[]{:S(2)}, u32[]{:S(2)}) %collective-permute-start.1) | collective-permute-done | bytes 270368 | tf_op jit(solution)/shard_map/ppermute | solution.py:201
  52.9 2.9 %collective-permute-done.2.c_ref = s16[32,4224]{1,0:T(8,128)(2,1)S(1)} collective-permute-done((s16[32,4224]{1,0:T(8,128)(2,1)S(1)}, s16[32,4224]{1,0:T(8,128)(2,1)S(1)}, u32[]{:S(2)}, u32[]{:S(2)}) %collective-permute-start.2) | collective-permute-done | bytes 270368 | tf_op jit(solution)/shard_map/ppermute | solution.py:201
  55.8 0.3 shard_map.71
  56.1 5.7 %collective-permute-start.4 = (s16[8,4224]{1,0:T(8,128)(2,1)S(1)}, s16[8,4224]{1,0:T(8,128)(2,1)S(1)}, u32[]{:S(2)}, u32[]{:S(2)}) collective-permute-start(s16[8,4224]{1,0:T(8,128)(2,1)S(1)} %get-tuple-element.28), channel_id=1, source_target_pairs={{0,128},{1,385},{2,130},{3,387},{4,132},{5,389},{6,134},{7,391},{8... | collective-permute-start | bytes 202760 | tf_op jit(solution)/shard_map/ppermute | solution.py:201
  61.8 3.5 %collective-permute-start.3 = (s16[8,4224]{1,0:T(8,128)(2,1)S(1)}, s16[8,4224]{1,0:T(8,128)(2,1)S(1)}, u32[]{:S(2)}, u32[]{:S(2)}) collective-permute-start(s16[8,4224]{1,0:T(8,128)(2,1)S(1)} %get-tuple-element.26), channel_id=1, source_target_pairs={{0,384},{1,129},{2,386},{3,131},{4,388},{5,133},{6,390},{7,135},{8... | collective-permute-start | bytes 202760 | tf_op jit(solution)/shard_map/ppermute | solution.py:201
  65.3 0.0 collective-permute-done.4.far_ref
  65.3 0.2 shard_map.72
  65.5 6.8 %collective-permute-start.5 = (s16[8,4224]{1,0:T(8,128)(2,1)S(1)}, s16[8,4224]{1,0:T(8,128)(2,1)S(1)}, u32[]{:S(2)}, u32[]{:S(2)}) collective-permute-start(s16[8,4224]{1,0:T(8,128)(2,1)S(1)} %shard_map.72), channel_id=1, source_target_pairs={{0,128},{1,385},{2,130},{3,387},{4,132},{5,389},{6,134},{7,391},{8... | collective-permute-start | bytes 202760 | tf_op jit(solution)/shard_map/ppermute | solution.py:201
  72.3 0.0 collective-permute-done.3.a_ref
  72.4 3.5 %collective-permute-done.5.b_ref = s16[8,4224]{1,0:T(8,128)(2,1)S(1)} collective-permute-done((s16[8,4224]{1,0:T(8,128)(2,1)S(1)}, s16[8,4224]{1,0:T(8,128)(2,1)S(1)}, u32[]{:S(2)}, u32[]{:S(2)}) %collective-permute-start.5) | collective-permute-done | bytes 67616 | tf_op jit(solution)/shard_map/ppermute | solution.py:201
  75.9 0.3 shard_map.73
  76.2 12.0 %all_to_all.15.stats_ref = f32[32,1,128]{2,1,0:T(1,128)S(1)} all-to-all(f32[32,1,128]{2,1,0:T(1,128)S(1)} %get-tuple-element.31), channel_id=1, replica_groups=mesh['rows'=16,'vocab'=32] {'vocab'}, dimensions={0} | all-to-all | bytes 32768 | tf_op jit(solution)/shard_map/all_to_all | solution.py:191
  88.2 0.9 shard_map.74
  (3 shorter events, 0.0 us)
Async XLA Ops:
  0.6 11.8 %copy-start = (s32[24,128]{1,0:T(8,128)S(1)}, s32[24,128]{1,0:T(8,128)}, u32[]{:S(2)}) copy-start(s32[24,128]{1,0:T(8,128)} %param.7) | copy-start | bytes 36868
  0.6 18.2 %all-to-all-start = ((bf16[32,16,128]{2,1,0:T(8,128)(2,1)}), bf16[32,16,128]{2,1,0:T(8,128)(2,1)S(1)}, u32[]{:S(2)}, u32[]{:S(2)}) async-start(bf16[32,16,128]{2,1,0:T(8,128)(2,1)} %bitcast.10), calls=%async_computation | async-start | bytes 262144 | tf_op jit(solution)/shard_map/all_to_all | solution.py:191
  19.5 11.7 %all-to-all-start.1 = ((bf16[32,16,128]{2,1,0:T(8,128)(2,1)}), bf16[32,16,128]{2,1,0:T(8,128)(2,1)S(1)}, u32[]{:S(2)}, u32[]{:S(2)}) async-start(bf16[32,16,128]{2,1,0:T(8,128)(2,1)} %shard_map.68), calls=%async_computation.1 | async-start | bytes 262144 | tf_op jit(solution)/shard_map/all_to_all | solution.py:191
  33.6 15.0 %collective-permute-start = (s16[32,4224]{1,0:T(8,128)(2,1)S(1)}, s16[32,4224]{1,0:T(8,128)(2,1)S(1)}, u32[]{:S(2)}, u32[]{:S(2)}) collective-permute-start(s16[32,4224]{1,0:T(8,128)(2,1)S(1)} %get-tuple-element.22), channel_id=1, source_target_pairs={{0,480},{1,33},{2,482},{3,35},{4,484},{5,37},{6,486},{7,39},{8,488... | collective-permute-start | bytes 811016 | tf_op jit(solution)/shard_map/ppermute | solution.py:201
  35.5 17.3 %collective-permute-start.1 = (s16[32,4224]{1,0:T(8,128)(2,1)S(1)}, s16[32,4224]{1,0:T(8,128)(2,1)S(1)}, u32[]{:S(2)}, u32[]{:S(2)}) collective-permute-start(s16[32,4224]{1,0:T(8,128)(2,1)S(1)} %get-tuple-element.23), channel_id=1, source_target_pairs={{0,64},{1,449},{2,66},{3,451},{4,68},{5,453},{6,70},{7,455},{8,72}... | collective-permute-start | bytes 811016 | tf_op jit(solution)/shard_map/ppermute | solution.py:201
  45.9 9.8 %collective-permute-start.2 = (s16[32,4224]{1,0:T(8,128)(2,1)S(1)}, s16[32,4224]{1,0:T(8,128)(2,1)S(1)}, u32[]{:S(2)}, u32[]{:S(2)}) collective-permute-start(s16[32,4224]{1,0:T(8,128)(2,1)S(1)} %get-tuple-element.24), channel_id=1, source_target_pairs={{0,32},{1,481},{2,34},{3,483},{4,36},{5,485},{6,38},{7,487},{8,40}... | collective-permute-start | bytes 811016 | tf_op jit(solution)/shard_map/ppermute | solution.py:201
  56.1 9.2 %collective-permute-start.4 = (s16[8,4224]{1,0:T(8,128)(2,1)S(1)}, s16[8,4224]{1,0:T(8,128)(2,1)S(1)}, u32[]{:S(2)}, u32[]{:S(2)}) collective-permute-start(s16[8,4224]{1,0:T(8,128)(2,1)S(1)} %get-tuple-element.28), channel_id=1, source_target_pairs={{0,128},{1,385},{2,130},{3,387},{4,132},{5,389},{6,134},{7,391},{8... | collective-permute-start | bytes 202760 | tf_op jit(solution)/shard_map/ppermute | solution.py:201
  61.8 10.5 %collective-permute-start.3 = (s16[8,4224]{1,0:T(8,128)(2,1)S(1)}, s16[8,4224]{1,0:T(8,128)(2,1)S(1)}, u32[]{:S(2)}, u32[]{:S(2)}) collective-permute-start(s16[8,4224]{1,0:T(8,128)(2,1)S(1)} %get-tuple-element.26), channel_id=1, source_target_pairs={{0,384},{1,129},{2,386},{3,131},{4,388},{5,133},{6,390},{7,135},{8... | collective-permute-start | bytes 202760 | tf_op jit(solution)/shard_map/ppermute | solution.py:201
  65.5 10.3 %collective-permute-start.5 = (s16[8,4224]{1,0:T(8,128)(2,1)S(1)}, s16[8,4224]{1,0:T(8,128)(2,1)S(1)}, u32[]{:S(2)}, u32[]{:S(2)}) collective-permute-start(s16[8,4224]{1,0:T(8,128)(2,1)S(1)} %shard_map.72), channel_id=1, source_target_pairs={{0,128},{1,385},{2,130},{3,387},{4,132},{5,389},{6,134},{7,391},{8... | collective-permute-start | bytes 202760 | tf_op jit(solution)/shard_map/ppermute | solution.py:201
